TPU v7x, 32 devices: a whole 2x2x4 slice. The times are simulated.
32 devices in a mesh: interval: 2 (over y), seq: 4 (over x, core), head: 4 (over z).
Axes of the slice: x: 2, y: 2, z: 4, core: 2. Of those that a mesh axis runs over, the one named last changes fastest.
Arguments:
- hidden_in: bfloat16 [2, 1024, 1536], P('interval', 'seq'), may hold values from -6 to 6
- ctx_grad: bfloat16 [2, 1024, 1536], P('interval', 'seq', 'head'), may hold values from -6 to 6
- w_query: bfloat16 [1536, 1536], P('head'), may hold values from -0.15625 to 0.15625
- w_key: bfloat16 [1536, 1536], P('head'), may hold values from -0.15625 to 0.15625
- w_value: bfloat16 [1536, 1536], P('head'), may hold values from -0.15625 to 0.15625
- w_junction: bfloat16 [1536, 128], replicated, may hold values from -0.15625 to 0.15625
- donor_pos: int32 [2, 4, 4, 32], P('interval', 'seq', None, 'head'), may hold values from 0 to 255
- acceptor_pos: int32 [2, 4, 4, 32], P('interval', 'seq', None, 'head'), may hold values from 0 to 255
- junction_counts: int32 [2, 4, 4], P('interval', 'seq'), may hold values from 8 to 32, as said below
- pred_grad: float32 [2, 4, 4, 32], P('interval', 'seq', None, 'head'), may hold values from -6 to 6
Outputs:
- grad_input: bfloat16 [2, 1024, 1536], P('interval', 'seq', 'head')
- grad_query: bfloat16 [1536, 1536], P('head')
- grad_key: bfloat16 [1536, 1536], P('head')
- grad_value: bfloat16 [1536, 1536], P('head')
Inputs may be any that keep to these rules, and one draw needn't show every extreme that they name: `junction_counts`: slots at or past a bucket's count are empty. In each interval one acceptor shard, drawn from the seed, has 32 live slots from every donor shard; every other bucket has 8 to 16.
All inputs are finite; a program needn't handle non-finite values.
Results may differ from a plain program's by a relative error of at most 0.022.
Values may be sent and summed in bfloat16 or wider, within the bound.
A program may use at most 64 MiB of HBM per device.

v0:
```python
import jax
import jax.numpy as jnp
from jax import lax
from jax.sharding import PartitionSpec as P

HD = 192
PJ = 128


def on_device(
    hidden_in,
    ctx_grad,
    w_query,
    w_key,
    w_value,
    w_junction,
    donor_pos,
    acceptor_pos,
    junction_counts,
    pred_grad,
):
    hidden = hidden_in[0]
    local_len = hidden.shape[0]
    shard_count = lax.axis_size("seq")
    total_len = local_len * shard_count
    heads_dev = w_query.shape[0] // HD
    softmax_scale = HD ** (-0.5)
    pair_scale = PJ ** (-0.5)
    queries = jnp.einsum("td,cd->tc", hidden, w_query, preferred_element_type=jnp.float32).astype(
        jnp.bfloat16
    )
    key_rows = jnp.einsum("td,cd->tc", hidden, w_key, preferred_element_type=jnp.float32).astype(
        jnp.bfloat16
    )
    value_rows = jnp.einsum(
        "td,cd->tc", hidden, w_value, preferred_element_type=jnp.float32
    ).astype(jnp.bfloat16)
    features = jnp.dot(hidden, w_junction, preferred_element_type=jnp.float32).astype(jnp.bfloat16)
    all_keys, all_values, all_features = (
        lax.all_gather(key_rows, "seq", axis=0, tiled=True),
        lax.all_gather(value_rows, "seq", axis=0, tiled=True),
        lax.all_gather(features, "seq", axis=0, tiled=True),
    )
    query_heads = queries.reshape(local_len, heads_dev, HD)
    grad_heads = ctx_grad[0].reshape(local_len, heads_dev, HD)
    key_heads = all_keys.reshape(total_len, heads_dev, HD)
    value_heads = all_values.reshape(total_len, heads_dev, HD)
    scores = (
        jnp.einsum("qhd,khd->hqk", query_heads, key_heads, preferred_element_type=jnp.float32)
        * softmax_scale
    )
    row_max = jnp.max(scores, axis=-1, keepdims=True)
    expd = jnp.exp(scores - row_max)
    probs = expd / jnp.sum(expd, axis=-1, keepdims=True)
    dprobs = jnp.einsum("qhd,khd->hqk", grad_heads, value_heads, preferred_element_type=jnp.float32)
    row_delta = jnp.sum(probs * dprobs, axis=-1, keepdims=True)
    dscores = probs * (dprobs - row_delta)
    probs_b = probs.astype(jnp.bfloat16)
    dscores_b = dscores.astype(jnp.bfloat16)
    query_grad = (
        (
            jnp.einsum("hqk,khd->qhd", dscores_b, key_heads, preferred_element_type=jnp.float32)
            * softmax_scale
        )
        .astype(jnp.bfloat16)
        .reshape(local_len, heads_dev * HD)
    )
    key_term = (
        jnp.einsum("hqk,qhd->khd", dscores_b, query_heads, preferred_element_type=jnp.float32)
        * softmax_scale
    ).reshape(total_len, heads_dev * HD)
    value_term = jnp.einsum(
        "hqk,qhd->khd", probs_b, grad_heads, preferred_element_type=jnp.float32
    ).reshape(total_len, heads_dev * HD)
    key_sum, value_sum = (
        lax.psum_scatter(
            key_term.astype(jnp.bfloat16), "seq", scatter_dimension=0, tiled=True
        ).astype(jnp.float32),
        lax.psum_scatter(
            value_term.astype(jnp.bfloat16), "seq", scatter_dimension=0, tiled=True
        ).astype(jnp.float32),
    )
    key_grad = key_sum.astype(jnp.bfloat16)
    value_grad = value_sum.astype(jnp.bfloat16)
    donor_idx = donor_pos[0, 0]
    accept_idx = acceptor_pos[0, 0]
    slot_dev = donor_idx.shape[1]
    slot_ids = lax.axis_index("head") * slot_dev + jnp.arange(slot_dev, dtype=jnp.int32)
    live_slots = slot_ids[None, :] < junction_counts[0, 0][:, None]
    donor_feat = features[donor_idx].astype(jnp.float32)
    accept_glob = jnp.arange(shard_count, dtype=jnp.int32)[:, None] * local_len + accept_idx
    accept_rows = all_features[accept_glob]
    accept_feat = accept_rows.astype(jnp.float32)
    pair_score = jnp.sum(donor_feat * accept_feat, axis=-1) * pair_scale
    slot_grad = (
        jnp.where(live_slots, pred_grad[0, 0] * jax.nn.sigmoid(pair_score), 0.0) * pair_scale
    )
    donor_term = slot_grad[..., None] * accept_feat
    accept_term = slot_grad[..., None] * donor_feat
    pair_width = features.shape[1]
    grad_feat = (
        jnp.zeros((local_len, pair_width), jnp.float32)
        .at[donor_idx.reshape(-1)]
        .add(donor_term.reshape(-1, pair_width))
    )
    spread_term = (
        jnp.zeros((total_len, pair_width), jnp.float32)
        .at[accept_glob.reshape(-1)]
        .add(accept_term.reshape(-1, pair_width))
    )
    grad_feat = grad_feat + lax.psum_scatter(
        spread_term.astype(jnp.bfloat16), "seq", scatter_dimension=0, tiled=True
    ).astype(jnp.float32)
    grad_feat_b = grad_feat.astype(jnp.bfloat16)
    input_term = jnp.einsum("tc,cd->td", query_grad, w_query, preferred_element_type=jnp.float32)
    input_term = input_term + jnp.einsum(
        "tc,cd->td", key_grad, w_key, preferred_element_type=jnp.float32
    )
    input_term = input_term + jnp.einsum(
        "tc,cd->td", value_grad, w_value, preferred_element_type=jnp.float32
    )
    input_term = input_term + jnp.einsum(
        "tp,dp->td", grad_feat_b, w_junction, preferred_element_type=jnp.float32
    )
    grad_input = lax.psum_scatter(
        input_term.astype(jnp.bfloat16), "head", scatter_dimension=1, tiled=True
    )
    key_wterm = jnp.einsum("tc,td->cd", key_grad, hidden, preferred_element_type=jnp.float32)
    value_wterm = jnp.einsum("tc,td->cd", value_grad, hidden, preferred_element_type=jnp.float32)
    query_wterm = jnp.einsum("tc,td->cd", query_grad, hidden, preferred_element_type=jnp.float32)
    query_wsum, key_wsum, value_wsum = lax.psum(
        (query_wterm, key_wterm, value_wterm), ("interval", "seq")
    )
    return (
        grad_input[None],
        query_wsum.astype(jnp.bfloat16),
        key_wsum.astype(jnp.bfloat16),
        value_wsum.astype(jnp.bfloat16),
    )


def solution(mesh):
    placed = (
        P("interval", "seq", None),
        P("interval", "seq", "head"),
        P("head", None),
        P("head", None),
        P("head", None),
        P(),
        P("interval", "seq", None, "head"),
        P("interval", "seq", None, "head"),
        P("interval", "seq", None),
        P("interval", "seq", None, "head"),
    )
    return jax.shard_map(
        on_device,
        mesh=mesh,
        in_specs=placed,
        out_specs=(P("interval", "seq", "head"), P("head", None), P("head", None), P("head", None)),
        check_vma=False,
    )
```

profile of v0, /device:TPU:0, one launch (start us, length us, event | category | flops | bytes accessed | tf_op | source)
XLA Modules:
  0.0 265.4 jit_solution(5917078045203630523)
XLA Ops:
  7.2 0.0 copy-start
  7.2 0.0 reduce-scatter.11.cloned.1.call-start
  7.3 0.8 squeeze.16
  8.1 0.8 squeeze.15
  8.9 0.1 lt.65
  9.0 0.8 compare_select_fusion
  9.7 0.1 reshape.237
  9.8 0.1 add.132
  9.9 0.1 add.133
  9.9 0.7 lt.67
  10.7 0.1 lt.68
  10.8 0.7 compare_select_fusion.1
  11.4 0.1 reshape.229
  11.6 0.0 copy-start.12
  11.6 0.0 copy-start.1
  11.6 1.7 convolution_convert_fusion.4
  13.3 7.2 %all_gather.11 = bf16[1024,128]{1,0:T(8,128)(2,1)S(1)} all-gather(bf16[256,128]{1,0:T(8,128)(2,1)S(1)} %convolution_convert_fusion.4), channel_id=1, replica_groups=mesh['interval'=2,'seq'=4,'head'=4] {'seq'}, dimensions={0}, use_global_device_ids=true | all-gather | bytes 327680 | tf_op jit(solution)/shard_map/all_gather | solution.py:42
  20.4 0.6 gather_fusion
  21.0 0.6 gather_fusion.1
  21.6 0.1 fusion.24
  21.8 0.9 scatter_custom_fusion
  22.7 0.7 convert_element_type.103
  23.4 0.0 reduce-scatter.11.cloned.1.call-update
  23.4 0.0 reduce-scatter.7.cloned.1.call-start
  23.5 0.8 copy.30
  24.3 0.6 convolution_convert_fusion.2
  24.9 0.8 copy.28
  25.8 0.6 convolution_convert_fusion.3
  26.3 0.7 copy-done.5
  27.0 0.6 convolution_convert_fusion.1
  27.6 8.7 %all_gather.10 = bf16[1024,384]{1,0:T(8,128)(2,1)S(1)} all-gather(bf16[256,384]{1,0:T(8,128)(2,1)S(1)} %convolution_convert_fusion.1), channel_id=1, replica_groups=mesh['interval'=2,'seq'=4,'head'=4] {'seq'}, dimensions={0}, use_global_device_ids=true | all-gather | bytes 983040 | tf_op jit(solution)/shard_map/all_gather | solution.py:41
  36.3 1.2 copy.29
  37.5 10.1 %all_gather.9 = bf16[1024,384]{1,0:T(8,128)(2,1)S(1)} all-gather(bf16[256,384]{1,0:T(8,128)(2,1)S(1)} %convolution_convert_fusion.3), channel_id=1, replica_groups=mesh['interval'=2,'seq'=4,'head'=4] {'seq'}, dimensions={0}, use_global_device_ids=true | all-gather | bytes 983040 | tf_op jit(solution)/shard_map/all_gather | solution.py:40
  47.6 0.3 copy.27
  47.9 0.0 copy-start.8
  47.9 0.0 copy-start.9
  47.9 3.4 %fusion.32 = (f32[2,256]{1,0:T(2,128)S(1)}, f32[2,256,1024]{2,1,0:T(8,128)}) fusion(bf16[256,2,192]{0,2,1:T(8,128)(2,1)} %bitcast.88, bf16[1024,2,192]{0,2,1:T(8,128)(2,1)S(1)} %bitcast.84), kind=kOutput, calls=%fused_computation.64 | convolution fusion | flops 202900480 | bytes 3082240 | tf_op jit(solution)/shard_map/sub | solution.py:53
  51.3 2.5 fusion.2
  53.8 0.4 fusion.4
  54.2 0.6 copy-done.10
  54.7 1.3 multiply_convert_fusion
  56.0 0.0 reduce-scatter.7.cloned.1.call-update
  56.0 0.0 reduce-scatter.9.cloned.1.call-start
  56.1 2.9 %convolution_convert_fusion = bf16[2,1024,192]{1,2,0:T(8,128)(2,1)} fusion(bf16[256,2,192]{0,2,1:T(8,128)(2,1)S(1)} %bitcast.91, f32[2,256,1024]{2,1,0:T(8,128)} %get-tuple-element.8, f32[2,256]{1,0:T(2,128)S(1)} %get-tuple-element.7), kind=kOutput, calls=%fused_computation.18 | convolution fusion | flops 202768384 | bytes 3082240 | tf_op jit(solution)/shard_map/hqk,qhd->khd/dot_general | solution.py:72
  59.0 0.0 reduce-scatter.9.cloned.1.call-update
  59.1 0.0 reduce-scatter.13.cloned.1.call-start
  59.1 0.1 reshape_squeeze.7
  59.2 1.6 fusion.6
  60.8 1.9 fusion.13
  62.7 0.6 fusion.33
  63.3 0.0 reduce-scatter.11.cloned.1.call-done
  63.4 1.5 convert_element_type.104
  64.9 2.3 scatter_custom_fusion.1
  67.2 13.6 %reduce-scatter.7.cloned.1.call-done = bf16[256,384]{0,1:T(8,128)(2,1)} async-done(((bf16[1024,384]{0,1:T(8,128)(2,1)}), bf16[256,384]{0,1:T(8,128)(2,1)}) %reduce-scatter.7.cloned.1.call-update) | async-done | bytes 196624 | tf_op jit(solution)/shard_map/reduce_scatter | solution.py:76
  80.7 3.1 %convolution_add_fusion.2 = f32[256,1536]{1,0:T(8,128)} fusion(f32[256,1536]{1,0:T(8,128)S(1)} %fusion.33, bf16[256,384]{0,1:T(8,128)(2,1)} %reduce-scatter.7.cloned.1.call-done, bf16[384,1536]{1,0:T(8,128)(2,1)} %param.13), kind=kOutput, calls=%fused_computation.7 | convolution fusion | flops 302383104 | bytes 4521984 | tf_op jit(solution)/shard_map/tc,cd->td/dot_general | solution.py:116
  83.9 23.3 %reduce-scatter.9.cloned.1.call-done = bf16[256,384]{0,1:T(8,128)(2,1)} async-done(((bf16[1024,384]{0,1:T(8,128)(2,1)}), bf16[256,384]{0,1:T(8,128)(2,1)}) %reduce-scatter.9.cloned.1.call-update) | async-done | bytes 196624 | tf_op jit(solution)/shard_map/reduce_scatter | solution.py:79
  107.2 2.4 convolution_add_fusion.1
  109.6 0.4 fusion.1
  110.0 1.1 copy.33
  111.1 0.0 reduce-scatter.13.cloned.1.call-update
  111.2 1.9 fusion.9
  113.1 1.9 fusion.11
  115.0 142.2 %all-reduce.2 = (bf16[384,1536]{1,0:T(8,128)(2,1)}, bf16[384,1536]{1,0:T(8,128)(2,1)}, bf16[384,1536]{1,0:T(8,128)(2,1)}) all-reduce(f32[384,1536]{1,0:T(8,128)} %fusion.13, f32[384,1536]{1,0:T(8,128)} %fusion.11, f32[384,1536]{1,0:T(8,128)} %fusion.9), channel_id=1, replica_groups=mesh['interval'=2,'seq'=4,'head'=4] {'interval','seq'}, use_global_device_ids=true, to_apply=%region_10.11 | all-reduce | flops 1769472 | bytes 10616832 | tf_op jit(solution)/shard_map/psum | solution.py:131
  257.2 1.7 copy.34
  (32 shorter events, 0.1 us)
Async XLA Ops:
  7.2 17.2 %copy-start = (bf16[384,1536]{1,0:T(8,128)(2,1)S(1)}, bf16[384,1536]{1,0:T(8,128)(2,1)}, u32[]{:S(2)}) copy-start(bf16[384,1536]{1,0:T(8,128)(2,1)} %param.12) | copy-start | bytes 3538948
  7.2 56.2 %reduce-scatter.11.cloned.1.call-start = ((), (), s32[]{:S(2)}) async-start(), calls=%async_computation.6 | async-start | bytes 327680 | tf_op jit(solution)/shard_map/reduce_scatter | solution.py:111
  11.6 11.9 %copy-start.12 = (bf16[1,256,384]{2,1,0:T(8,128)(2,1)S(1)}, bf16[1,256,384]{2,1,0:T(8,128)(2,1)}, u32[]{:S(2)}) copy-start(bf16[1,256,384]{2,1,0:T(8,128)(2,1)} %param.11) | copy-start | bytes 589828
  11.6 12.8 %copy-start.1 = (bf16[1,256,1536]{2,1,0:T(8,128)(2,1)S(1)}, bf16[1,256,1536]{2,1,0:T(8,128)(2,1)}, u32[]{:S(2)}) copy-start(bf16[1,256,1536]{2,1,0:T(8,128)(2,1)} %param.10) | copy-start | bytes 2359300
  23.4 2.3 copy-start.4
  23.4 57.3 %reduce-scatter.7.cloned.1.call-start = ((), (), s32[]{:S(2)}) async-start(), calls=%async_computation.4 | async-start | bytes 983040 | tf_op jit(solution)/shard_map/reduce_scatter | solution.py:76
  25.7 1.3 copy-start.5
  47.9 3.4 %copy-start.8 = (bf16[1024,384]{0,1:T(8,128)(2,1)}, bf16[1024,384]{0,1:T(8,128)(2,1)S(1)}, u32[]{:S(2)}) copy-start(bf16[1024,384]{0,1:T(8,128)(2,1)S(1)} %copy.27) | copy-start | bytes 2359300
  47.9 3.4 %copy-start.9 = (bf16[1024,384]{0,1:T(8,128)(2,1)S(1)}, bf16[1024,384]{0,1:T(8,128)(2,1)}, u32[]{:S(2)}) copy-start(bf16[1024,384]{0,1:T(8,128)(2,1)} %copy.29) | copy-start | bytes 2359300
  51.3 2.5 copy-start.2
  53.8 0.9 copy-start.10
  54.7 1.3 copy-start.13
  56.0 3.1 %copy-start.14 = (s32[1,1,4,8]{3,2,1,0:T(4,128)S(1)}, s32[1,1,4,8]{3,2,1,0:T(4,128)}, u32[]{:S(2)}) copy-start(s32[1,1,4,8]{3,2,1,0:T(4,128)} %param.16) | copy-start | bytes 388
  56.0 51.1 %reduce-scatter.9.cloned.1.call-start = ((), (), s32[]{:S(2)}) async-start(), calls=%async_computation.5 | async-start | bytes 983040 | tf_op jit(solution)/shard_map/reduce_scatter | solution.py:79
  59.1 198.1 %reduce-scatter.13.cloned.1.call-start = ((), (), s32[]{:S(2)}) async-start(), calls=%async_computation.7 | async-start | bytes 983040
  83.9 25.7 %copy-start.3 = (bf16[1536,128]{1,0:T(8,128)(2,1)S(1)}, bf16[1536,128]{1,0:T(8,128)(2,1)}, u32[]{:S(2)}) copy-start(bf16[1536,128]{1,0:T(8,128)(2,1)} %param.15) | copy-start | bytes 1179652
  83.9 25.7 %copy-start.11 = (f32[256,128]{1,0:T(8,128)S(1)}, f32[256,128]{1,0:T(8,128)}, u32[]{:S(2)}) copy-start(f32[256,128]{1,0:T(8,128)} %scatter_custom_fusion.1) | copy-start | bytes 393220
  110.0 1.2 copy-start.7
  111.2 1.9 copy-start.6
Sparse Core Ops, SparseCore 0:
  23.6 22.6 reduce-scatter.10
  56.1 24.5 reduce-scatter.6
  83.9 23.2 reduce-scatter.8
  111.3 23.2 reduce-scatter.12
where the time goes:
time: 266 us; the launch traced here: 265 us
  blocking collectives  168 us (63%)
  waiting for transfers between devices  36.9 us (14%)
  matrix products  27.3 us (10%)
  between operations  14 us (5%)
  local copies, waits for them, and re-layouts  11.4 us (4%)
  other arithmetic  7.4 us (3%)
    psum x1, blocking collectives, on_device(): lax.psum((query_wterm, key_wterm, value_wterm), ('interval', 'seq'))  142 us
    reduce_scatter x1, waiting for transfers between devices, on_device(): lax.psum_scatter(value_term.astype(jnp.bfloat16), 'seq', scatter_dimensio...  23.3 us
    reduce_scatter x1, waiting for transfers between devices, on_device(): lax.psum_scatter(key_term.astype(jnp.bfloat16), 'seq', scatter_dimension=...  13.6 us
    all_gather x1, blocking collectives, on_device(): lax.all_gather(key_rows, 'seq', axis=0, tiled=True)  10.1 us
    all_gather x1, blocking collectives, on_device(): lax.all_gather(value_rows, 'seq', axis=0, tiled=True)  8.71 us
    all_gather x1, blocking collectives, on_device(): lax.all_gather(features, 'seq', axis=0, tiled=True)  7.19 us
  transfers between devices with their start and end apart: 4, of which 2 were waited for; matrix products, arithmetic and copies ran while one was open for 11% of the time, Pallas kernels for 0%

commit v1 on v0

--- a/solution.py
+++ b/solution.py
@@ -1,10 +1,451 @@
+import functools
+
 import jax
 import jax.numpy as jnp
 from jax import lax
+from jax.experimental import pallas as pl
+from jax.experimental.pallas import tpu as pltpu
 from jax.sharding import PartitionSpec as P
 
 HD = 192
 PJ = 128
+MESH = pl.DeviceIdType.MESH
+F32 = jnp.float32
+BF16 = jnp.bfloat16
+
+
+def dot_nn(a, b):
+    return lax.dot_general(a, b, (((1,), (0,)), ((), ())), preferred_element_type=F32)
+
+
+def dot_nt(a, b):
+    return lax.dot_general(a, b, (((1,), (1,)), ((), ())), preferred_element_type=F32)
+
+
+def dot_tn(a, b):
+    return lax.dot_general(a, b, (((0,), (0,)), ((), ())), preferred_element_type=F32)
+
+
+def fused_kernel(
+    n_head,
+    n_copies,
+    hid,
+    ctx,
+    wq,
+    wk,
+    wv,
+    wj,
+    slots,
+    out_in,
+    out_q,
+    out_k,
+    out_v,
+    kbuf,
+    vbuf,
+    fbuf,
+    slotbuf,
+    qbuf,
+    hid_sib,
+    sref,
+    dpref,
+    pb,
+    dsb,
+    term,
+    from_sib,
+    pair_sum,
+    from_xn,
+    own_term,
+    grads,
+    grads_sib,
+    dwp,
+    rs1,
+    s1,
+    rs2,
+    zsend,
+    zrecv,
+    zown,
+    send_sems,
+    recv_sems,
+):
+    toks = hid.shape[0]
+    width = hid.shape[1]
+    feats = wq.shape[0]
+    heads = feats // HD
+    half = width // 2
+    quart = half // 2
+    row_half = feats // 2
+    row_q = feats // 4
+    scale = HD**-0.5
+    iv = lax.axis_index("interval")
+    sq = lax.axis_index("seq")
+    hd = lax.axis_index("head")
+    xi = lax.div(sq, 2)
+    core = lax.rem(sq, 2)
+    s_sib = sq + 1 - 2 * core
+    s_xn = lax.rem(sq + 2, 4)
+    s_dg = lax.rem(s_sib + 2, 4)
+    sib = (iv, s_sib, hd)
+    xn = (iv, s_xn, hd)
+    yn = (1 - iv, sq, hd)
+    zpeers = [(iv, sq, lax.rem(hd + d, n_head)) for d in range(1, n_head)]
+
+    counter = [0]
+    started = []
+
+    def send(src, dst, dev):
+        i = counter[0]
+        counter[0] += 1
+        copy = pltpu.make_async_remote_copy(
+            src_ref=src,
+            dst_ref=dst,
+            send_sem=send_sems.at[i],
+            recv_sem=recv_sems.at[i],
+            device_id=dev,
+            device_id_type=MESH,
+        )
+        copy.start()
+        started.append(copy)
+        return copy
+
+    barrier = pltpu.get_barrier_semaphore()
+    for dev in [sib, xn, yn] + zpeers:
+        pl.semaphore_signal(barrier, inc=1, device_id=dev, device_id_type=MESH)
+
+    kbuf[0] = dot_nt(hid[...], wk[...]).astype(BF16)
+    pl.semaphore_wait(barrier, 3 + len(zpeers))
+    k_xn = send(kbuf.at[0], kbuf.at[2], xn)
+    k_sib = send(kbuf.at[0], kbuf.at[1], sib)
+    vbuf[0] = dot_nt(hid[...], wv[...]).astype(BF16)
+    v_xn = send(vbuf.at[0], vbuf.at[2], xn)
+    v_sib = send(vbuf.at[0], vbuf.at[1], sib)
+    fbuf[0] = dot_nn(hid[...], wj[...]).astype(BF16)
+    slotbuf[0] = slots[...]
+    f_xn = send(fbuf.at[0], fbuf.at[2], xn)
+    f_sib = send(fbuf.at[0], fbuf.at[1], sib)
+    t_xn = send(slotbuf.at[0], slotbuf.at[2], xn)
+    t_sib = send(slotbuf.at[0], slotbuf.at[1], sib)
+    other_half = pl.ds(pl.multiple_of((1 - core) * half, half), half)
+    my_half = pl.ds(pl.multiple_of(core * half, half), half)
+    h_sib = send(hid.at[:, other_half], hid_sib, sib)
+    qbuf[...] = dot_nt(hid[...], wq[...]).astype(BF16)
+
+    def head_cols(h):
+        return slice(h * HD, (h + 1) * HD)
+
+    def block_cols(r):
+        return slice(r * toks, (r + 1) * toks)
+
+    def scores(r):
+        for h in range(heads):
+            sref[h, :, block_cols(r)] = dot_nt(qbuf[:, head_cols(h)], kbuf[r, :, head_cols(h)])
+
+    def dprobs(r):
+        for h in range(heads):
+            dpref[h, :, block_cols(r)] = dot_nt(ctx[:, head_cols(h)], vbuf[r, :, head_cols(h)])
+
+    scores(0)
+    dprobs(0)
+    k_sib.wait_recv()
+    scores(1)
+    k_xn.wait_recv()
+    k_fw = send(kbuf.at[2], kbuf.at[3], sib)
+    scores(2)
+    k_fw.wait_recv()
+    scores(3)
+
+    rows_step = 32
+
+    for h in range(heads):
+
+        @pl.loop(0, toks // rows_step)
+        def _(i, h=h):
+            rows = pl.ds(pl.multiple_of(i * rows_step, rows_step), rows_step)
+            raw = sref[h, rows, :] * scale
+            e = jnp.exp(raw - jnp.max(raw, axis=-1, keepdims=True))
+            p = e / jnp.sum(e, axis=-1, keepdims=True)
+            sref[h, rows, :] = p
+            pb[h, rows, :] = p.astype(BF16)
+
+    def kv_terms(which, left, right, factor):
+        def one(r):
+            parts = [
+                dot_tn(left[h, :, block_cols(r)], right[:, head_cols(h)]) for h in range(heads)
+            ]
+            full = jnp.concatenate(parts, axis=-1)
+            return full * factor if factor != 1.0 else full
+
+        term[which, 0] = one(3).astype(BF16)
+        a = send(term.at[which, 0], from_sib.at[which, 0], sib)
+        term[which, 1] = one(1).astype(BF16)
+        b = send(term.at[which, 1], from_sib.at[which, 1], sib)
+        mine = one(2)
+        a.wait_recv()
+        pair_sum[which] = (mine + from_sib[which, 0].astype(F32)).astype(BF16)
+        c = send(pair_sum.at[which], from_xn.at[which], xn)
+        own_term[which] = one(0)
+        return b, c
+
+    def kv_final(which, slot, b, c):
+        b.wait_recv()
+        c.wait_recv()
+        total = own_term[which] + from_sib[which, 1].astype(F32) + from_xn[which].astype(F32)
+        grads[slot] = total.astype(BF16)
+        return send(grads.at[slot], grads_sib.at[slot], sib)
+
+    v_pend = kv_terms(1, pb, ctx, 1.0)
+    v_sib.wait_recv()
+    dprobs(1)
+    v_xn.wait_recv()
+    v_fw = send(vbuf.at[2], vbuf.at[3], sib)
+    f_xn.wait_recv()
+    f_fw = send(fbuf.at[2], fbuf.at[3], sib)
+    t_xn.wait_recv()
+    t_fw = send(slotbuf.at[2], slotbuf.at[3], sib)
+    dprobs(2)
+    v_fw.wait_recv()
+    dprobs(3)
+
+    for h in range(heads):
+
+        @pl.loop(0, toks // rows_step)
+        def _(i, h=h):
+            rows = pl.ds(pl.multiple_of(i * rows_step, rows_step), rows_step)
+            p = sref[h, rows, :]
+            dp = dpref[h, rows, :]
+            delta = jnp.sum(p * dp, axis=-1, keepdims=True)
+            dsb[h, rows, :] = (p * (dp - delta)).astype(BF16)
+
+    k_pend = kv_terms(0, dsb, qbuf, scale)
+
+    q_parts = []
+    for h in range(heads):
+        acc = dot_nn(dsb[h, :, block_cols(0)], kbuf[0, :, head_cols(h)])
+        for r in range(1, 4):
+            acc = acc + dot_nn(dsb[h, :, block_cols(r)], kbuf[r, :, head_cols(h)])
+        q_parts.append(acc * scale)
+    grads[0] = jnp.concatenate(q_parts, axis=-1).astype(BF16)
+    g_copy = [None] * 3
+    g_copy[0] = send(grads.at[0], grads_sib.at[0], sib)
+
+    outs = (out_q, out_k, out_v)
+
+    first_pos = (xi, iv)
+    second_pos = (iv, xi)
+    first_dev = (xn, yn)
+    second_dev = (yn, xn)
+    rs1_copy = {}
+    rs2_copy = {}
+    ag1_copy = {}
+    ag2_copy = {}
+    sib_copy = []
+
+    def part_lanes(p):
+        return pl.ds(pl.multiple_of(core * half + p * quart, 128), quart)
+
+    def half_rows(p, mine):
+        pos = first_pos[p] if mine else 1 - first_pos[p]
+        return pl.ds(pl.multiple_of(pos * row_half, 16), row_half)
+
+    def quarter_rows(p):
+        return pl.ds(
+            pl.multiple_of(first_pos[p] * row_half + second_pos[p] * row_q, 16), row_q
+        )
+
+    def dw_start(w):
+        g_copy[w].wait_recv()
+        for p in (1, 0):
+            lanes = part_lanes(p)
+            mine = dot_tn(grads[w], hid[:, lanes])
+            theirs = dot_tn(grads_sib[w], hid_sib[:, p * quart : (p + 1) * quart])
+            dwp[w, p] = (mine + theirs).astype(BF16)
+            rs1_copy[w, p] = send(dwp.at[w, p, half_rows(p, False)], rs1.at[w, p], first_dev[p])
+
+    def dw_second(w):
+        for p in (1, 0):
+            rs1_copy[w, p].wait_recv()
+            own = dwp[w, p, half_rows(p, True), :].astype(F32)
+            s1[w, p] = (own + rs1[w, p].astype(F32)).astype(BF16)
+            away = pl.ds(pl.multiple_of((1 - second_pos[p]) * row_q, 16), row_q)
+            rs2_copy[w, p] = send(s1.at[w, p, away], rs2.at[w, p], second_dev[p])
+
+    def dw_gather1(w):
+        for p in (1, 0):
+            rs2_copy[w, p].wait_recv()
+            keep = pl.ds(pl.multiple_of(second_pos[p] * row_q, 16), row_q)
+            done = s1[w, p, keep, :].astype(F32) + rs2[w, p].astype(F32)
+            outs[w][quarter_rows(p), part_lanes(p)] = done.astype(BF16)
+            piece = outs[w].at[quarter_rows(p), part_lanes(p)]
+            ag1_copy[w, p] = send(piece, piece, second_dev[p])
+
+    def dw_gather2(w):
+        for p in (1, 0):
+            ag1_copy[w, p].wait_recv()
+            piece = outs[w].at[half_rows(p, True), part_lanes(p)]
+            ag2_copy[w, p] = send(piece, piece, first_dev[p])
+            sib_copy.append(send(piece, piece, sib))
+
+    def dw_last(w):
+        for p in (1, 0):
+            ag2_copy[w, p].wait_recv()
+            piece = outs[w].at[half_rows(p, False), part_lanes(p)]
+            sib_copy.append(send(piece, piece, sib))
+
+    h_sib.wait_recv()
+    dw_start(0)
+
+    g_copy[2] = kv_final(1, 2, *v_pend)
+
+    f_sib.wait_recv()
+    t_sib.wait_recv()
+    f_fw.wait_recv()
+    t_fw.wait_recv()
+    rows_all = slotbuf[0] + slotbuf[1] + slotbuf[2] + slotbuf[3]
+    donor_row = rows_all[0:1, :]
+    accept_row = rows_all[1:2, :]
+    pred_row = rows_all[2:3, :]
+    n_slots = rows_all.shape[1]
+    tok_iota = lax.broadcasted_iota(jnp.int32, (toks, n_slots), 0)
+    own_donor = None
+    own_accept = None
+    donor_t = jnp.zeros((PJ, n_slots), F32)
+    accept_t = jnp.zeros((PJ, n_slots), F32)
+    for r, shard in enumerate((sq, s_sib, s_xn, s_dg)):
+        tok = (tok_iota + shard * toks).astype(F32)
+        hot_d = jnp.where(tok == donor_row, 1.0, 0.0).astype(BF16)
+        hot_a = jnp.where(tok == accept_row, 1.0, 0.0).astype(BF16)
+        if r == 0:
+            own_donor, own_accept = hot_d, hot_a
+        donor_t = donor_t + dot_tn(fbuf[r], hot_d)
+        accept_t = accept_t + dot_tn(fbuf[r], hot_a)
+    pair_scale = PJ**-0.5
+    pair = jnp.sum(donor_t * accept_t, axis=0, keepdims=True) * pair_scale
+    slot_grad = pred_row * (1.0 / (1.0 + jnp.exp(-pair))) * pair_scale
+    grad_feat = dot_nt(own_donor, (slot_grad * accept_t).astype(BF16)) + dot_nt(
+        own_accept, (slot_grad * donor_t).astype(BF16)
+    )
+    grad_feat = grad_feat.astype(BF16)
+
+    dw_start(2)
+    dw_second(0)
+    g_copy[1] = kv_final(0, 1, *k_pend)
+    dw_start(1)
+
+    cols = width // n_head
+    z_copy = []
+
+    def input_block(owner):
+        lanes = pl.ds(pl.multiple_of(owner * cols, 128), cols)
+        acc = dot_nn(grads[0], wq[:, lanes]) + dot_nn(grads[1], wk[:, lanes])
+        acc = acc + dot_nn(grads[2], wv[:, lanes])
+        wj_rows = wj[pl.ds(pl.multiple_of(owner * cols, 128), cols), :]
+        return acc + dot_nt(grad_feat, wj_rows)
+
+    for d in range(n_head - 1, 0, -1):
+        zsend[d - 1] = input_block(lax.rem(hd + d, n_head)).astype(BF16)
+        z_copy.append((d, send(zsend.at[d - 1], zrecv.at[d - 1], zpeers[d - 1])))
+        if d == n_head - 1:
+            dw_second(2)
+        elif d == n_head - 2:
+            dw_gather1(0)
+    zown[...] = input_block(hd)
+    dw_second(1)
+    dw_gather1(2)
+    dw_gather2(0)
+    dw_gather1(1)
+    dw_gather2(2)
+    dw_last(0)
+    dw_gather2(1)
+    for d, copy in z_copy:
+        copy.wait_recv()
+    total = zown[...]
+    for d in range(n_head - 1):
+        total = total + zrecv[d].astype(F32)
+    out_in[...] = total.astype(BF16)
+    dw_last(2)
+    dw_last(1)
+    for copy in sib_copy:
+        copy.wait_recv()
+    for copy in started:
+        copy.wait_send()
+    assert counter[0] == n_copies
+
+
+def fused_device(
+    n_head,
+    hidden_in,
+    ctx_grad,
+    w_query,
+    w_key,
+    w_value,
+    w_junction,
+    donor_pos,
+    acceptor_pos,
+    junction_counts,
+    pred_grad,
+):
+    hidden = hidden_in[0]
+    toks, width = hidden.shape
+    feats = w_query.shape[0]
+    heads = feats // HD
+    n_seq = 4
+    sq = lax.axis_index("seq")
+    slot_dev = donor_pos.shape[3]
+    slot_ids = lax.axis_index("head") * slot_dev + jnp.arange(slot_dev, dtype=jnp.int32)
+    live = slot_ids[None, :] < junction_counts[0, 0][:, None]
+    donor = (donor_pos[0, 0] + sq * toks).astype(F32)
+    accept = (acceptor_pos[0, 0] + jnp.arange(n_seq, dtype=jnp.int32)[:, None] * toks).astype(F32)
+    pred = jnp.where(live, pred_grad[0, 0], 0.0)
+    n_own = n_seq * slot_dev
+    packed = jnp.stack([donor, accept, pred]).reshape(3, 1, n_own)
+    place = (jnp.arange(n_seq) == sq).reshape(1, n_seq, 1)
+    packed = jnp.where(place, packed, 0.0).reshape(3, n_seq * n_own)
+    slots = jnp.concatenate([packed, jnp.zeros((5, n_seq * n_own), F32)], axis=0)
+    n_slots = n_seq * n_own
+    n_copies = 58 + n_head - 1
+    vmem = pl.BlockSpec(memory_space=pltpu.VMEM)
+    half, quart = width // 2, width // 4
+    cols = width // n_head
+    scratch = [
+        pltpu.VMEM((4, toks, feats), BF16),
+        pltpu.VMEM((4, toks, feats), BF16),
+        pltpu.VMEM((4, toks, PJ), BF16),
+        pltpu.VMEM((4, 8, n_slots), F32),
+        pltpu.VMEM((toks, feats), BF16),
+        pltpu.VMEM((toks, half), BF16),
+        pltpu.VMEM((heads, toks, 4 * toks), F32),
+        pltpu.VMEM((heads, toks, 4 * toks), F32),
+        pltpu.VMEM((heads, toks, 4 * toks), BF16),
+        pltpu.VMEM((heads, toks, 4 * toks), BF16),
+        pltpu.VMEM((2, 2, toks, feats), BF16),
+        pltpu.VMEM((2, 2, toks, feats), BF16),
+        pltpu.VMEM((2, toks, feats), BF16),
+        pltpu.VMEM((2, toks, feats), BF16),
+        pltpu.VMEM((2, toks, feats), F32),
+        pltpu.VMEM((3, toks, feats), BF16),
+        pltpu.VMEM((3, toks, feats), BF16),
+        pltpu.VMEM((3, 2, feats, quart), BF16),
+        pltpu.VMEM((3, 2, feats // 2, quart), BF16),
+        pltpu.VMEM((3, 2, feats // 2, quart), BF16),
+        pltpu.VMEM((3, 2, feats // 4, quart), BF16),
+        pltpu.VMEM((n_head - 1, toks, cols), BF16),
+        pltpu.VMEM((n_head - 1, toks, cols), BF16),
+        pltpu.VMEM((toks, cols), F32),
+        pltpu.SemaphoreType.DMA((n_copies,)),
+        pltpu.SemaphoreType.DMA((n_copies,)),
+    ]
+    grad_w = jax.ShapeDtypeStruct((feats, width), BF16)
+    out_in, out_q, out_k, out_v = pl.pallas_call(
+        functools.partial(fused_kernel, n_head, n_copies),
+        out_shape=(jax.ShapeDtypeStruct((toks, cols), BF16), grad_w, grad_w, grad_w),
+        in_specs=[vmem] * 7,
+        out_specs=(vmem,) * 4,
+        scratch_shapes=scratch,
+        compiler_params=pltpu.CompilerParams(
+            collective_id=0, has_side_effects=True, vmem_limit_bytes=56 * 1024 * 1024
+        ),
+        name="attention_backward",
+    )(hidden, ctx_grad[0], w_query, w_key, w_value, w_junction, slots)
+    return out_in[None], out_q, out_k, out_v
 
 
 def on_device(
@@ -152,8 +593,11 @@
         P("interval", "seq", None),
         P("interval", "seq", None, "head"),
     )
+    shape = dict(mesh.shape)
+    fits = shape["interval"] == 2 and shape["seq"] == 4 and shape["head"] == 4
+    run = functools.partial(fused_device, shape["head"]) if fits else on_device
     return jax.shard_map(
-        on_device,
+        run,
         mesh=mesh,
         in_specs=placed,
         out_specs=(P("interval", "seq", "head"), P("head", None), P("head", None), P("head", None)),

time: 266 us -> 76.4 us (0.29)
  blocking collectives: 168 us -> 0 us
  Pallas kernels: 0 us -> 64.4 us
  waiting for transfers between devices: 36.9 us -> 0 us
  matrix products: 27.3 us -> 0 us
  between operations: 14 us -> 0.68 us
  other arithmetic: 7.4 us -> 0.73 us
    psum x1 -> x0, blocking collectives: 142 us -> none  [on_device(): lax.psum((query_wterm, key_wterm, value_wterm), ('interval', 'seq'))]
    pallas_call x0 -> x1, Pallas kernels: none -> 64.4 us  [fused_device(): pl.pallas_call(functools.partial(fused_kernel, n_head, n_copies), out_sha...]
    reduce_scatter x3 -> x0, waiting for transfers between devices: 36.9 us -> none  [the longest x1 23.3 us: on_device(): lax.psum_scatter(value_term.astype(jnp.bfloat16), 'seq', scatter_dimensio...]
    all_gather x3 -> x0, blocking collectives: 26 us -> none  [the longest x1 10.1 us: on_device(): lax.all_gather(key_rows, 'seq', axis=0, tiled=True)]
    dot_general x15 -> x0, matrix products: 23.9 us -> none  [the longest x1 3.14 us: on_device(): jnp.einsum('tc,cd->td', key_grad, w_key, preferred_element_type=jnp.float32)]
    sub x1 -> x0, matrix products: 3.4 us -> none  [on_device(): expd = jnp.exp(scores - row_max)]
    scatter-add x2 -> x0, other arithmetic: 3.22 us -> none  [the longest x1 2.31 us: on_device(): grad_feat = jnp.zeros((local_len, pair_width), jnp.float32).at[donor_idx....]
    unnamed x33 -> x9, local copies, waits for them, and re-layouts: 5.01 us -> 6.8 us
  transfers between devices with their start and end apart: 4 -> 0, of which waited for: 2 -> 0; matrix products, arithmetic and copies ran while one was open for 11% -> 0% of each run, Pallas kernels for 0% -> 0%
where the time goes in v1:
time: 76.4 us; the launch traced here: 76.1 us
  Pallas kernels  64.4 us (84%)
  local copies, waits for them, and re-layouts  10.3 us (13%)
    pallas_call x1, Pallas kernels, fused_device(): pl.pallas_call(functools.partial(fused_kernel, n_head, n_copies), out_sha...  64.4 us
    unnamed x9, local copies, waits for them, and re-layouts  6.8 us

profile of v1, /device:TPU:0, one launch (start us, length us, event | category | flops | bytes accessed | tf_op | source)
XLA Modules:
  0.0 76.1 jit_solution(13572747191775647562)
XLA Ops:
  0.6 0.1 broadcast_in_dim.38
  0.7 0.1 broadcast_in_dim.39
  0.8 0.8 %squeeze.15 = s32[1,1,32]{2,1,0:T(1,128)S(1)} reshape(s32[1,1,4,8]{3,2,1,0:T(4,128)} %param.17) | data formatting | bytes 256 | tf_op jit(solution)/shard_map/squeeze | solution.py:396
  1.6 0.8 %squeeze.16 = f32[1,1,32]{2,1,0:T(1,128)S(1)} reshape(f32[1,1,4,8]{3,2,1,0:T(4,128)} %param.19) | data formatting | bytes 256 | tf_op jit(solution)/shard_map/squeeze | solution.py:397
  2.3 0.1 add.47
  2.4 0.1 add.48
  2.5 0.7 add_convert_fusion
  3.2 0.1 convert_element_type.26
  3.3 0.1 lt.28
  3.4 0.7 lt.30
  4.1 0.1 lt.31
  4.2 0.1 broadcast_in_dim.44
  4.3 0.6 concatenate.4.slots
  4.9 64.4 %attention_backward.1 = (bf16[256,384]{1,0:T(8,128)(2,1)}, bf16[384,1536]{1,0:T(8,128)(2,1)}, bf16[384,1536]{1,0:T(8,128)(2,1)}, bf16[384,1536]{1,0:T(8,128)(2,1)}) custom-call(bf16[256,1536]{1,0:T(8,128)(2,1)} %bitcast.11, bf16[256,384]{1,0:T(8,128)(2,1)} %bitcast.12, bf16[384,1536]{1,0:T(8,128)(2,1)} %wq.1, bf16[384,1536]{1,0:T(8,128)(2,1)} %wk.1, ...), custom_call_target="tpu_custom_call" | custom-call | tf_op jit(solution)/shard_map/attention_backward/pallas_call | solution.py:437
  69.3 1.6 %copy.21 = bf16[1,256,384]{2,1,0:T(8,128)(2,1)} copy(bf16[1,256,384]{2,1,0:T(8,128)(2,1)} %bitcast.13) | data formatting | bytes 393216
  70.9 0.0 copy-start.1
  70.9 2.5 %copy.22 = bf16[384,1536]{1,0:T(8,128)(2,1)} copy(bf16[384,1536]{1,0:T(8,128)(2,1)} %get-tuple-element.17) | data formatting | bytes 2359296
  73.4 0.0 copy-done.1
  73.4 0.0 copy-start
  73.4 1.0 %copy.23 = bf16[384,1536]{1,0:T(8,128)(2,1)} copy(bf16[384,1536]{1,0:T(8,128)(2,1)S(1)} %copy-done.1) | data formatting | bytes 2359296
  74.4 0.7 copy-done
  75.1 1.0 %copy.24 = bf16[384,1536]{1,0:T(8,128)(2,1)} copy(bf16[384,1536]{1,0:T(8,128)(2,1)S(1)} %copy-done) | data formatting | bytes 2359296
  (10 shorter events, 0.0 us)
Async XLA Ops:
  70.9 2.5 %copy-start.1 = (bf16[384,1536]{1,0:T(8,128)(2,1)S(1)}, bf16[384,1536]{1,0:T(8,128)(2,1)}, u32[]{:S(2)}) copy-start(bf16[384,1536]{1,0:T(8,128)(2,1)} %get-tuple-element.18) | copy-start | bytes 3538948
  73.4 1.7 %copy-start = (bf16[384,1536]{1,0:T(8,128)(2,1)S(1)}, bf16[384,1536]{1,0:T(8,128)(2,1)}, u32[]{:S(2)}) copy-start(bf16[384,1536]{1,0:T(8,128)(2,1)} %get-tuple-element.19) | copy-start | bytes 3538948

commit v2 on v1

--- a/solution.py
+++ b/solution.py
@@ -29,13 +29,26 @@
 def fused_kernel(
     n_head,
     n_copies,
-    hid,
+    hid_hbm,
+    ctx_hbm,
+    wq_hbm,
+    wk_hbm,
+    wv_hbm,
+    wj_hbm,
+    donor,
+    accept,
+    counts,
+    pred,
+    in_hbm,
+    q_hbm,
+    k_hbm,
+    v_hbm,
+    hidbuf,
     ctx,
     wq,
     wk,
     wv,
     wj,
-    slots,
     out_in,
     out_q,
     out_k,
@@ -45,7 +58,8 @@
     fbuf,
     slotbuf,
     qbuf,
-    hid_sib,
+    q_t,
+    ctx_t,
     sref,
     dpref,
     pb,
@@ -56,25 +70,26 @@
     from_xn,
     own_term,
     grads,
-    grads_sib,
+    grads_t,
+    gcat,
     dwp,
-    rs1,
-    s1,
-    rs2,
+    rsum,
     zsend,
     zrecv,
     zown,
     send_sems,
     recv_sems,
+    load_sems,
+    store_sems,
 ):
-    toks = hid.shape[0]
-    width = hid.shape[1]
+    toks = ctx.shape[0]
+    width = hidbuf.shape[1]
     feats = wq.shape[0]
     heads = feats // HD
     half = width // 2
-    quart = half // 2
-    row_half = feats // 2
-    row_q = feats // 4
+    row_y = feats // 2
+    row_c = feats // 4
+    row_x = feats // 8
     scale = HD**-0.5
     iv = lax.axis_index("interval")
     sq = lax.axis_index("seq")
@@ -87,7 +102,24 @@
     sib = (iv, s_sib, hd)
     xn = (iv, s_xn, hd)
     yn = (1 - iv, sq, hd)
+    ysib = (1 - iv, s_sib, hd)
     zpeers = [(iv, sq, lax.rem(hd + d, n_head)) for d in range(1, n_head)]
+    hid = hidbuf.at[0:toks]
+
+    loads = []
+    for i, (src, dst) in enumerate(
+        (
+            (hid_hbm.at[0], hid),
+            (wk_hbm, wk),
+            (wv_hbm, wv),
+            (wq_hbm, wq),
+            (wj_hbm, wj),
+            (ctx_hbm.at[0], ctx),
+        )
+    ):
+        load = pltpu.make_async_copy(src, dst, load_sems.at[i])
+        load.start()
+        loads.append(load)
 
     counter = [0]
     started = []
@@ -107,27 +139,63 @@
         started.append(copy)
         return copy
 
+    stores = []
+
+    def store(src, dst):
+        copy = pltpu.make_async_copy(src, dst, store_sems.at[len(stores)])
+        copy.start()
+        stores.append(copy)
+
     barrier = pltpu.get_barrier_semaphore()
-    for dev in [sib, xn, yn] + zpeers:
+    peers = [sib, xn, yn, ysib] + zpeers
+    for dev in peers:
         pl.semaphore_signal(barrier, inc=1, device_id=dev, device_id_type=MESH)
 
+    loads[0].wait()
+    loads[1].wait()
     kbuf[0] = dot_nt(hid[...], wk[...]).astype(BF16)
-    pl.semaphore_wait(barrier, 3 + len(zpeers))
+    pl.semaphore_wait(barrier, len(peers))
     k_xn = send(kbuf.at[0], kbuf.at[2], xn)
     k_sib = send(kbuf.at[0], kbuf.at[1], sib)
+    hid_yn = []
+    for p in range(2):
+        lanes = slice(p * half, (p + 1) * half)
+        hid_yn.append(send(hidbuf.at[0:toks, lanes], hidbuf.at[2 * toks : 3 * toks, lanes], yn))
+    loads[2].wait()
     vbuf[0] = dot_nt(hid[...], wv[...]).astype(BF16)
     v_xn = send(vbuf.at[0], vbuf.at[2], xn)
     v_sib = send(vbuf.at[0], vbuf.at[1], sib)
+    loads[3].wait()
+    q_full = dot_nt(hid[...], wq[...])
+    qbuf[...] = q_full.astype(BF16)
+    q_t[...] = jnp.transpose(q_full).astype(BF16)
+    loads[4].wait()
     fbuf[0] = dot_nn(hid[...], wj[...]).astype(BF16)
-    slotbuf[0] = slots[...]
     f_xn = send(fbuf.at[0], fbuf.at[2], xn)
     f_sib = send(fbuf.at[0], fbuf.at[1], sib)
+
+    n_acc, slot_dev = donor.shape[2], donor.shape[3]
+    n_slots = slotbuf.shape[2]
+    acc_iota = lax.broadcasted_iota(jnp.int32, (n_acc, slot_dev), 0)
+    slot_ids = lax.broadcasted_iota(jnp.int32, (n_acc, slot_dev), 1) + hd * slot_dev
+    live_count = jnp.zeros((n_acc, slot_dev), jnp.int32)
+    for j in range(n_acc):
+        live_count = jnp.where(acc_iota == j, counts[0, :, j : j + 1], live_count)
+    donor_tok = (donor[0, 0] + sq * toks).astype(F32)
+    accept_tok = (accept[0, 0] + acc_iota * toks).astype(F32)
+    pred_live = jnp.where(slot_ids < live_count, pred[0, 0], 0.0)
+    lane_iota = lax.broadcasted_iota(jnp.int32, (n_acc, n_slots), 1)
+    row_iota = lax.broadcasted_iota(jnp.int32, (n_acc, n_slots), 0)
+    place = lane_iota - (sq * n_acc + row_iota) * slot_dev
+    slotbuf[0] = jnp.zeros(slotbuf.shape[1:], F32)
+    for i, values in enumerate((donor_tok, accept_tok, pred_live)):
+        spread = jnp.zeros((n_acc, n_slots), F32)
+        for j in range(slot_dev):
+            spread = jnp.where(place == j, values[:, j : j + 1], spread)
+        slotbuf[0, i : i + 1, :] = jnp.sum(spread, axis=0, keepdims=True)
     t_xn = send(slotbuf.at[0], slotbuf.at[2], xn)
     t_sib = send(slotbuf.at[0], slotbuf.at[1], sib)
-    other_half = pl.ds(pl.multiple_of((1 - core) * half, half), half)
-    my_half = pl.ds(pl.multiple_of(core * half, half), half)
-    h_sib = send(hid.at[:, other_half], hid_sib, sib)
-    qbuf[...] = dot_nt(hid[...], wq[...]).astype(BF16)
+    hid_sib = send(hidbuf.at[0:toks], hidbuf.at[toks : 2 * toks], sib)
 
     def head_cols(h):
         return slice(h * HD, (h + 1) * HD)
@@ -144,6 +212,8 @@
             dpref[h, :, block_cols(r)] = dot_nt(ctx[:, head_cols(h)], vbuf[r, :, head_cols(h)])
 
     scores(0)
+    loads[5].wait()
+    ctx_t[...] = jnp.transpose(ctx[...].astype(F32)).astype(BF16)
     dprobs(0)
     k_sib.wait_recv()
     scores(1)
@@ -166,41 +236,53 @@
             sref[h, rows, :] = p
             pb[h, rows, :] = p.astype(BF16)
 
-    def kv_terms(which, left, right, factor):
-        def one(r):
-            parts = [
-                dot_tn(left[h, :, block_cols(r)], right[:, head_cols(h)]) for h in range(heads)
-            ]
-            full = jnp.concatenate(parts, axis=-1)
-            return full * factor if factor != 1.0 else full
-
-        term[which, 0] = one(3).astype(BF16)
+    def kv_terms(which, left_t, right, factor):
+        def one(h, r):
+            part = dot_nn(left_t[head_cols(h), :], right[h, :, block_cols(r)])
+            return part * factor if factor != 1.0 else part
+
+        for h in range(heads):
+            term[which, 0, head_cols(h), :] = one(h, 3).astype(BF16)
         a = send(term.at[which, 0], from_sib.at[which, 0], sib)
-        term[which, 1] = one(1).astype(BF16)
+        for h in range(heads):
+            term[which, 1, head_cols(h), :] = one(h, 1).astype(BF16)
         b = send(term.at[which, 1], from_sib.at[which, 1], sib)
-        mine = one(2)
+        for h in range(heads):
+            own_term[which, head_cols(h), :] = one(h, 2)
         a.wait_recv()
-        pair_sum[which] = (mine + from_sib[which, 0].astype(F32)).astype(BF16)
+        pair_sum[which] = (own_term[which] + from_sib[which, 0].astype(F32)).astype(BF16)
         c = send(pair_sum.at[which], from_xn.at[which], xn)
-        own_term[which] = one(0)
+        for h in range(heads):
+            own_term[which, head_cols(h), :] = one(h, 0)
         return b, c
+
+    def g_rows(y, c):
+        return pl.ds(pl.multiple_of(y * row_y + c * row_c, 16), row_c)
+
+    g_copy = [None] * 3
+
+    def exchange(slot):
+        gcat[slot, :, 0:toks] = grads_t[slot, g_rows(iv, core), :]
+        copies = []
+        for b, dev, y, c in ((2, yn, 1 - iv, core), (3, ysib, 1 - iv, 1 - core), (1, sib, iv, 1 - core)):
+            copies.append(
+                send(grads_t.at[slot, g_rows(y, c)], gcat.at[slot, :, block_cols(b)], dev)
+            )
+        g_copy[slot] = copies
 
     def kv_final(which, slot, b, c):
         b.wait_recv()
         c.wait_recv()
         total = own_term[which] + from_sib[which, 1].astype(F32) + from_xn[which].astype(F32)
-        grads[slot] = total.astype(BF16)
-        return send(grads.at[slot], grads_sib.at[slot], sib)
-
-    v_pend = kv_terms(1, pb, ctx, 1.0)
+        grads_t[slot] = total.astype(BF16)
+        exchange(slot)
+        grads[slot] = jnp.transpose(total).astype(BF16)
+
+    v_pend = kv_terms(1, ctx_t, pb, 1.0)
     v_sib.wait_recv()
     dprobs(1)
     v_xn.wait_recv()
     v_fw = send(vbuf.at[2], vbuf.at[3], sib)
-    f_xn.wait_recv()
-    f_fw = send(fbuf.at[2], fbuf.at[3], sib)
-    t_xn.wait_recv()
-    t_fw = send(slotbuf.at[2], slotbuf.at[3], sib)
     dprobs(2)
     v_fw.wait_recv()
     dprobs(3)
@@ -215,7 +297,7 @@
             delta = jnp.sum(p * dp, axis=-1, keepdims=True)
             dsb[h, rows, :] = (p * (dp - delta)).astype(BF16)
 
-    k_pend = kv_terms(0, dsb, qbuf, scale)
+    k_pend = kv_terms(0, q_t, dsb, scale)
 
     q_parts = []
     for h in range(heads):
@@ -223,77 +305,93 @@
         for r in range(1, 4):
             acc = acc + dot_nn(dsb[h, :, block_cols(r)], kbuf[r, :, head_cols(h)])
         q_parts.append(acc * scale)
-    grads[0] = jnp.concatenate(q_parts, axis=-1).astype(BF16)
-    g_copy = [None] * 3
-    g_copy[0] = send(grads.at[0], grads_sib.at[0], sib)
+    q_grad = jnp.concatenate(q_parts, axis=-1)
+    grads_t[0] = jnp.transpose(q_grad).astype(BF16)
+    exchange(0)
+    grads[0] = q_grad.astype(BF16)
+
+    f_xn.wait_recv()
+    f_fw = send(fbuf.at[2], fbuf.at[3], sib)
+    t_xn.wait_recv()
+    t_fw = send(slotbuf.at[2], slotbuf.at[3], sib)
+    hid_fw = []
+    for p in range(2):
+        lanes = slice(p * half, (p + 1) * half)
+        hid_yn[p].wait_recv()
+        hid_fw.append(
+            send(hidbuf.at[2 * toks : 3 * toks, lanes], hidbuf.at[3 * toks : 4 * toks, lanes], sib)
+        )
 
     outs = (out_q, out_k, out_v)
-
-    first_pos = (xi, iv)
-    second_pos = (iv, xi)
-    first_dev = (xn, yn)
-    second_dev = (yn, xn)
-    rs1_copy = {}
-    rs2_copy = {}
-    ag1_copy = {}
-    ag2_copy = {}
-    sib_copy = []
-
-    def part_lanes(p):
-        return pl.ds(pl.multiple_of(core * half + p * quart, 128), quart)
-
-    def half_rows(p, mine):
-        pos = first_pos[p] if mine else 1 - first_pos[p]
-        return pl.ds(pl.multiple_of(pos * row_half, 16), row_half)
-
-    def quarter_rows(p):
-        return pl.ds(
-            pl.multiple_of(first_pos[p] * row_half + second_pos[p] * row_q, 16), row_q
-        )
+    outs_hbm = (q_hbm, k_hbm, v_hbm)
+    pos = (xi, iv)
+    rs_copy = {}
+    piece_copy = {}
+    fwd_copy = {}
+    sib_copy = {0: [], 1: [], 2: []}
+
+    def x_rows(x):
+        return pl.ds(pl.multiple_of(x * row_x, 16), row_x)
+
+    def piece(w, p, y, x):
+        start = pl.multiple_of(y * row_y + core * row_c + x * row_x, 16)
+        return outs[w].at[pl.ds(start, row_x), slice(p * half, (p + 1) * half)]
+
+    def to_sib(w, ref):
+        sib_copy[w].append(send(ref, ref, sib))
 
     def dw_start(w):
-        g_copy[w].wait_recv()
-        for p in (1, 0):
-            lanes = part_lanes(p)
-            mine = dot_tn(grads[w], hid[:, lanes])
-            theirs = dot_tn(grads_sib[w], hid_sib[:, p * quart : (p + 1) * quart])
-            dwp[w, p] = (mine + theirs).astype(BF16)
-            rs1_copy[w, p] = send(dwp.at[w, p, half_rows(p, False)], rs1.at[w, p], first_dev[p])
-
-    def dw_second(w):
-        for p in (1, 0):
-            rs1_copy[w, p].wait_recv()
-            own = dwp[w, p, half_rows(p, True), :].astype(F32)
-            s1[w, p] = (own + rs1[w, p].astype(F32)).astype(BF16)
-            away = pl.ds(pl.multiple_of((1 - second_pos[p]) * row_q, 16), row_q)
-            rs2_copy[w, p] = send(s1.at[w, p, away], rs2.at[w, p], second_dev[p])
-
-    def dw_gather1(w):
-        for p in (1, 0):
-            rs2_copy[w, p].wait_recv()
-            keep = pl.ds(pl.multiple_of(second_pos[p] * row_q, 16), row_q)
-            done = s1[w, p, keep, :].astype(F32) + rs2[w, p].astype(F32)
-            outs[w][quarter_rows(p), part_lanes(p)] = done.astype(BF16)
-            piece = outs[w].at[quarter_rows(p), part_lanes(p)]
-            ag1_copy[w, p] = send(piece, piece, second_dev[p])
-
-    def dw_gather2(w):
-        for p in (1, 0):
-            ag1_copy[w, p].wait_recv()
-            piece = outs[w].at[half_rows(p, True), part_lanes(p)]
-            ag2_copy[w, p] = send(piece, piece, first_dev[p])
-            sib_copy.append(send(piece, piece, sib))
+        for copy in g_copy[w]:
+            copy.wait_recv()
+        for p in range(2):
+            dwp[w, p] = dot_nn(gcat[w], hidbuf[:, p * half : (p + 1) * half]).astype(BF16)
+            rs_copy[w, p] = send(dwp.at[w, p, x_rows(1 - xi)], rsum.at[w, p], xn)
+
+    def dw_final(w):
+        for p in range(2):
+            rs_copy[w, p].wait_recv()
+            done = dwp[w, p, x_rows(xi), :].astype(F32) + rsum[w, p].astype(F32)
+            ref = piece(w, p, iv, xi)
+            ref[...] = done.astype(BF16)
+            cx = send(ref, ref, xn)
+            cy = send(ref, ref, yn)
+            piece_copy[w, p] = (cx, cy)
+            to_sib(w, ref)
+
+    def dw_forward(w):
+        for p in range(2):
+            cx, cy = piece_copy[w, p]
+            cx_ref = piece(w, p, iv, 1 - xi)
+            cy_ref = piece(w, p, 1 - iv, xi)
+            if p == 0:
+                cx.wait_recv()
+                fwd_copy[w, p] = send(cx_ref, cx_ref, yn)
+                to_sib(w, cx_ref)
+                cy.wait_recv()
+                to_sib(w, cy_ref)
+            else:
+                cy.wait_recv()
+                fwd_copy[w, p] = send(cy_ref, cy_ref, xn)
+                to_sib(w, cy_ref)
+                cx.wait_recv()
+                to_sib(w, cx_ref)
 
     def dw_last(w):
-        for p in (1, 0):
-            ag2_copy[w, p].wait_recv()
-            piece = outs[w].at[half_rows(p, False), part_lanes(p)]
-            sib_copy.append(send(piece, piece, sib))
-
-    h_sib.wait_recv()
+        for p in range(2):
+            fwd_copy[w, p].wait_recv()
+            to_sib(w, piece(w, p, 1 - iv, 1 - xi))
+
+    def dw_out(w):
+        for copy in sib_copy[w]:
+            copy.wait_recv()
+        store(outs[w], outs_hbm[w])
+
+    kv_final(1, 2, *v_pend)
+    hid_sib.wait_recv()
+    hid_fw[0].wait_recv()
+    hid_fw[1].wait_recv()
     dw_start(0)
-
-    g_copy[2] = kv_final(1, 2, *v_pend)
+    dw_start(2)
 
     f_sib.wait_recv()
     t_sib.wait_recv()
@@ -303,7 +401,6 @@
     donor_row = rows_all[0:1, :]
     accept_row = rows_all[1:2, :]
     pred_row = rows_all[2:3, :]
-    n_slots = rows_all.shape[1]
     tok_iota = lax.broadcasted_iota(jnp.int32, (toks, n_slots), 0)
     own_donor = None
     own_accept = None
@@ -325,9 +422,8 @@
     )
     grad_feat = grad_feat.astype(BF16)
 
-    dw_start(2)
-    dw_second(0)
-    g_copy[1] = kv_final(0, 1, *k_pend)
+    kv_final(0, 1, *k_pend)
+    dw_final(0)
     dw_start(1)
 
     cols = width // n_head
@@ -337,37 +433,45 @@
         lanes = pl.ds(pl.multiple_of(owner * cols, 128), cols)
         acc = dot_nn(grads[0], wq[:, lanes]) + dot_nn(grads[1], wk[:, lanes])
         acc = acc + dot_nn(grads[2], wv[:, lanes])
-        wj_rows = wj[pl.ds(pl.multiple_of(owner * cols, 128), cols), :]
-        return acc + dot_nt(grad_feat, wj_rows)
+        return acc + dot_nt(grad_feat, wj[lanes, :])
 
     for d in range(n_head - 1, 0, -1):
         zsend[d - 1] = input_block(lax.rem(hd + d, n_head)).astype(BF16)
         z_copy.append((d, send(zsend.at[d - 1], zrecv.at[d - 1], zpeers[d - 1])))
         if d == n_head - 1:
-            dw_second(2)
-        elif d == n_head - 2:
-            dw_gather1(0)
+            dw_final(2)
     zown[...] = input_block(hd)
-    dw_second(1)
-    dw_gather1(2)
-    dw_gather2(0)
-    dw_gather1(1)
-    dw_gather2(2)
+    dw_forward(0)
+    dw_final(1)
+    dw_forward(2)
     dw_last(0)
-    dw_gather2(1)
+    dw_forward(1)
+    dw_last(2)
+    dw_out(0)
+    dw_last(1)
     for d, copy in z_copy:
         copy.wait_recv()
     total = zown[...]
     for d in range(n_head - 1):
         total = total + zrecv[d].astype(F32)
     out_in[...] = total.astype(BF16)
-    dw_last(2)
-    dw_last(1)
-    for copy in sib_copy:
-        copy.wait_recv()
+    store(out_in, in_hbm.at[0])
+    dw_out(2)
+    dw_out(1)
     for copy in started:
         copy.wait_send()
-    assert counter[0] == n_copies
+    for copy in stores:
+        copy.wait()
+    assert counter[0] <= n_copies
+
+
+def write_kernel(*refs):
+    n = 4
+    copies = [pltpu.make_async_copy(refs[i], refs[n + i], refs[2 * n].at[i]) for i in range(n)]
+    for copy in copies:
+        copy.start()
+    for copy in copies:
+        copy.wait()
 
 
 def fused_device(
@@ -383,69 +487,88 @@
     junction_counts,
     pred_grad,
 ):
-    hidden = hidden_in[0]
-    toks, width = hidden.shape
+    toks, width = hidden_in.shape[1:]
     feats = w_query.shape[0]
     heads = feats // HD
     n_seq = 4
-    sq = lax.axis_index("seq")
-    slot_dev = donor_pos.shape[3]
-    slot_ids = lax.axis_index("head") * slot_dev + jnp.arange(slot_dev, dtype=jnp.int32)
-    live = slot_ids[None, :] < junction_counts[0, 0][:, None]
-    donor = (donor_pos[0, 0] + sq * toks).astype(F32)
-    accept = (acceptor_pos[0, 0] + jnp.arange(n_seq, dtype=jnp.int32)[:, None] * toks).astype(F32)
-    pred = jnp.where(live, pred_grad[0, 0], 0.0)
-    n_own = n_seq * slot_dev
-    packed = jnp.stack([donor, accept, pred]).reshape(3, 1, n_own)
-    place = (jnp.arange(n_seq) == sq).reshape(1, n_seq, 1)
-    packed = jnp.where(place, packed, 0.0).reshape(3, n_seq * n_own)
-    slots = jnp.concatenate([packed, jnp.zeros((5, n_seq * n_own), F32)], axis=0)
-    n_slots = n_seq * n_own
-    n_copies = 58 + n_head - 1
+    n_slots = n_seq * donor_pos.shape[2] * donor_pos.shape[3]
+    n_copies = 96
     vmem = pl.BlockSpec(memory_space=pltpu.VMEM)
-    half, quart = width // 2, width // 4
+    hbm = pl.BlockSpec(memory_space=pl.ANY)
+    half = width // 2
     cols = width // n_head
     scratch = [
+        pltpu.VMEM((4 * toks, width), BF16),
+        pltpu.VMEM((toks, feats), BF16),
+        pltpu.VMEM((feats, width), BF16),
+        pltpu.VMEM((feats, width), BF16),
+        pltpu.VMEM((feats, width), BF16),
+        pltpu.VMEM((width, PJ), BF16),
+        pltpu.VMEM((toks, cols), BF16),
+        pltpu.VMEM((feats, width), BF16),
+        pltpu.VMEM((feats, width), BF16),
+        pltpu.VMEM((feats, width), BF16),
         pltpu.VMEM((4, toks, feats), BF16),
         pltpu.VMEM((4, toks, feats), BF16),
         pltpu.VMEM((4, toks, PJ), BF16),
         pltpu.VMEM((4, 8, n_slots), F32),
         pltpu.VMEM((toks, feats), BF16),
-        pltpu.VMEM((toks, half), BF16),
+        pltpu.VMEM((feats, toks), BF16),
+        pltpu.VMEM((feats, toks), BF16),
         pltpu.VMEM((heads, toks, 4 * toks), F32),
         pltpu.VMEM((heads, toks, 4 * toks), F32),
         pltpu.VMEM((heads, toks, 4 * toks), BF16),
         pltpu.VMEM((heads, toks, 4 * toks), BF16),
-        pltpu.VMEM((2, 2, toks, feats), BF16),
-        pltpu.VMEM((2, 2, toks, feats), BF16),
-        pltpu.VMEM((2, toks, feats), BF16),
-        pltpu.VMEM((2, toks, feats), BF16),
-        pltpu.VMEM((2, toks, feats), F32),
+        pltpu.VMEM((2, 2, feats, toks), BF16),
+        pltpu.VMEM((2, 2, feats, toks), BF16),
+        pltpu.VMEM((2, feats, toks), BF16),
+        pltpu.VMEM((2, feats, toks), BF16),
+        pltpu.VMEM((2, feats, toks), F32),
         pltpu.VMEM((3, toks, feats), BF16),
-        pltpu.VMEM((3, toks, feats), BF16),
-        pltpu.VMEM((3, 2, feats, quart), BF16),
-        pltpu.VMEM((3, 2, feats // 2, quart), BF16),
-        pltpu.VMEM((3, 2, feats // 2, quart), BF16),
-        pltpu.VMEM((3, 2, feats // 4, quart), BF16),
+        pltpu.VMEM((3, feats, toks), BF16),
+        pltpu.VMEM((3, feats // 4, 4 * toks), BF16),
+        pltpu.VMEM((3, 2, feats // 4, half), BF16),
+        pltpu.VMEM((3, 2, feats // 8, half), BF16),
         pltpu.VMEM((n_head - 1, toks, cols), BF16),
         pltpu.VMEM((n_head - 1, toks, cols), BF16),
         pltpu.VMEM((toks, cols), F32),
         pltpu.SemaphoreType.DMA((n_copies,)),
         pltpu.SemaphoreType.DMA((n_copies,)),
+        pltpu.SemaphoreType.DMA((6,)),
+        pltpu.SemaphoreType.DMA((4,)),
     ]
     grad_w = jax.ShapeDtypeStruct((feats, width), BF16)
-    out_in, out_q, out_k, out_v = pl.pallas_call(
+    shapes = (jax.ShapeDtypeStruct((1, toks, cols), BF16), grad_w, grad_w, grad_w)
+    results = pl.pallas_call(
         functools.partial(fused_kernel, n_head, n_copies),
-        out_shape=(jax.ShapeDtypeStruct((toks, cols), BF16), grad_w, grad_w, grad_w),
-        in_specs=[vmem] * 7,
-        out_specs=(vmem,) * 4,
+        out_shape=shapes,
+        in_specs=[hbm] * 6 + [vmem] * 4,
+        out_specs=(hbm,) * 4,
         scratch_shapes=scratch,
         compiler_params=pltpu.CompilerParams(
             collective_id=0, has_side_effects=True, vmem_limit_bytes=56 * 1024 * 1024
         ),
         name="attention_backward",
-    )(hidden, ctx_grad[0], w_query, w_key, w_value, w_junction, slots)
-    return out_in[None], out_q, out_k, out_v
+    )(
+        hidden_in,
+        ctx_grad,
+        w_query,
+        w_key,
+        w_value,
+        w_junction,
+        donor_pos,
+        acceptor_pos,
+        junction_counts,
+        pred_grad,
+    )
+    return pl.pallas_call(
+        write_kernel,
+        out_shape=shapes,
+        in_specs=[hbm] * 4,
+        out_specs=(hbm,) * 4,
+        scratch_shapes=[pltpu.SemaphoreType.DMA((4,))],
+        name="write_results",
+    )(*results)
 
 
 def on_device(

time: 76.4 us -> 175 us (2.29)
  Pallas kernels: 64.4 us -> 174 us
  local copies, waits for them, and re-layouts: 10.3 us -> 0 us
    pallas_call x0 -> x1, Pallas kernels: none -> 114 us  [fused_device(): pl.pallas_call(write_kernel, out_shape=shapes, in_specs=[hbm] * 4, out_sp...]
    unnamed x9 -> x0, local copies, waits for them, and re-layouts: 6.8 us -> none
    pallas_call x1, Pallas kernels: 64.4 us -> 60.1 us  [fused_device(): pl.pallas_call(functools.partial(fused_kernel, n_head, n_copies), out_sha...]
where the time goes in v2:
time: 175 us
  Pallas kernels  174 us (99%)
    pallas_call x1, Pallas kernels, fused_device(): pl.pallas_call(write_kernel, out_shape=shapes, in_specs=[hbm] * 4, out_sp...  114 us
    pallas_call x1, Pallas kernels, fused_device(): pl.pallas_call(functools.partial(fused_kernel, n_head, n_copies), out_sha...  60.1 us

profile of v2, /device:TPU:0, one launch (start us, length us, event | category | flops | bytes accessed | tf_op | source)
XLA Modules:
  0.0 175.1 jit_solution(5381943846091872556)
XLA Ops:
  0.6 60.1 %attention_backward.1 = (bf16[1,256,384]{2,1,0:T(8,128)(2,1)}, bf16[384,1536]{1,0:T(8,128)(2,1)}, bf16[384,1536]{1,0:T(8,128)(2,1)}, bf16[384,1536]{1,0:T(8,128)(2,1)}) custom-call(bf16[1,256,1536]{2,1,0:T(8,128)(2,1)} %hid_hbm.1, bf16[1,256,384]{2,1,0:T(8,128)(2,1)} %ctx_hbm.1, bf16[384,1536]{1,0:T(8,128)(2,1)} %wq_hbm.1, bf16[384,1536]{1,0:T(8,128)(2,1)} %wk_hbm.1, ...), custom_call_target="tpu_custom_call" | custom-call | tf_op jit(solution)/shard_map/attention_backward/pallas_call | solution.py:542
  60.8 114.3 %write_results.1 = (bf16[1,256,384]{2,1,0:T(8,128)(2,1)}, bf16[384,1536]{1,0:T(8,128)(2,1)}, bf16[384,1536]{1,0:T(8,128)(2,1)}, bf16[384,1536]{1,0:T(8,128)(2,1)}) custom-call(bf16[1,256,384]{2,1,0:T(8,128)(2,1)} %get-tuple-element.8.refs_0_, bf16[384,1536]{1,0:T(8,128)(2,1)} %get-tuple-element.9.refs_1_, bf16[384,1536]{1,0:T(8,128)(2,1)} %get-tuple-element.10.refs_2_, ...), custom_call_target="tpu_custom_call" | custom-call | tf_op jit(solution)/shard_map/write_results/pallas_call | solution.py:564

commit v3 on v2

--- a/solution.py
+++ b/solution.py
@@ -39,10 +39,10 @@
     accept,
     counts,
     pred,
-    in_hbm,
     q_hbm,
     k_hbm,
     v_hbm,
+    in_hbm,
     hidbuf,
     ctx,
     wq,
@@ -104,7 +104,14 @@
     yn = (1 - iv, sq, hd)
     ysib = (1 - iv, s_sib, hd)
     zpeers = [(iv, sq, lax.rem(hd + d, n_head)) for d in range(1, n_head)]
+    zpair = (iv, sq, hd + 1 - 2 * lax.rem(hd, 2))
+    split = toks // 2
+    mine_z = lax.rem(hd, 2) * split
     hid = hidbuf.at[0:toks]
+
+    def z_rows(base):
+        return pl.ds(pl.multiple_of(base + mine_z, 16), split)
+
 
     loads = []
     for i, (src, dst) in enumerate(
@@ -160,7 +167,9 @@
     hid_yn = []
     for p in range(2):
         lanes = slice(p * half, (p + 1) * half)
-        hid_yn.append(send(hidbuf.at[0:toks, lanes], hidbuf.at[2 * toks : 3 * toks, lanes], yn))
+        hid_yn.append(
+            send(hidbuf.at[z_rows(0), lanes], hidbuf.at[z_rows(2 * toks), lanes], yn)
+        )
     loads[2].wait()
     vbuf[0] = dot_nt(hid[...], wv[...]).astype(BF16)
     v_xn = send(vbuf.at[0], vbuf.at[2], xn)
@@ -171,7 +180,7 @@
     q_t[...] = jnp.transpose(q_full).astype(BF16)
     loads[4].wait()
     fbuf[0] = dot_nn(hid[...], wj[...]).astype(BF16)
-    f_xn = send(fbuf.at[0], fbuf.at[2], xn)
+    f_xn = send(fbuf.at[0, z_rows(0)], fbuf.at[2, z_rows(0)], xn)
     f_sib = send(fbuf.at[0], fbuf.at[1], sib)
 
     n_acc, slot_dev = donor.shape[2], donor.shape[3]
@@ -278,11 +287,23 @@
         exchange(slot)
         grads[slot] = jnp.transpose(total).astype(BF16)
 
+    def pass_on(arrived, ref):
+        arrived.wait_recv()
+        return send(ref, ref, zpair)
+
+    def hid_lanes(p):
+        return slice(p * half, (p + 1) * half)
+
+    hid_z = [pass_on(hid_yn[0], hidbuf.at[z_rows(2 * toks), hid_lanes(0)])]
     v_pend = kv_terms(1, ctx_t, pb, 1.0)
     v_sib.wait_recv()
     dprobs(1)
     v_xn.wait_recv()
     v_fw = send(vbuf.at[2], vbuf.at[3], sib)
+    hid_z.append(pass_on(hid_yn[1], hidbuf.at[z_rows(2 * toks), hid_lanes(1)]))
+    f_z = pass_on(f_xn, fbuf.at[2, z_rows(0)])
+    t_xn.wait_recv()
+    t_fw = send(slotbuf.at[2], slotbuf.at[3], sib)
     dprobs(2)
     v_fw.wait_recv()
     dprobs(3)
@@ -310,21 +331,18 @@
     exchange(0)
     grads[0] = q_grad.astype(BF16)
 
-    f_xn.wait_recv()
+    f_z.wait_recv()
     f_fw = send(fbuf.at[2], fbuf.at[3], sib)
-    t_xn.wait_recv()
-    t_fw = send(slotbuf.at[2], slotbuf.at[3], sib)
     hid_fw = []
     for p in range(2):
-        lanes = slice(p * half, (p + 1) * half)
-        hid_yn[p].wait_recv()
+        lanes = hid_lanes(p)
+        hid_z[p].wait_recv()
         hid_fw.append(
             send(hidbuf.at[2 * toks : 3 * toks, lanes], hidbuf.at[3 * toks : 4 * toks, lanes], sib)
         )
 
     outs = (out_q, out_k, out_v)
     outs_hbm = (q_hbm, k_hbm, v_hbm)
-    pos = (xi, iv)
     rs_copy = {}
     piece_copy = {}
     fwd_copy = {}
@@ -360,21 +378,14 @@
 
     def dw_forward(w):
         for p in range(2):
-            cx, cy = piece_copy[w, p]
+            cx = piece_copy[w, p][0]
             cx_ref = piece(w, p, iv, 1 - xi)
-            cy_ref = piece(w, p, 1 - iv, xi)
-            if p == 0:
-                cx.wait_recv()
-                fwd_copy[w, p] = send(cx_ref, cx_ref, yn)
-                to_sib(w, cx_ref)
-                cy.wait_recv()
-                to_sib(w, cy_ref)
-            else:
-                cy.wait_recv()
-                fwd_copy[w, p] = send(cy_ref, cy_ref, xn)
-                to_sib(w, cy_ref)
-                cx.wait_recv()
-                to_sib(w, cx_ref)
+            cx.wait_recv()
+            fwd_copy[w, p] = send(cx_ref, cx_ref, yn)
+            to_sib(w, cx_ref)
+        for p in range(2):
+            piece_copy[w, p][1].wait_recv()
+            to_sib(w, piece(w, p, 1 - iv, xi))
 
     def dw_last(w):
         for p in range(2):
@@ -455,7 +466,7 @@
     for d in range(n_head - 1):
         total = total + zrecv[d].astype(F32)
     out_in[...] = total.astype(BF16)
-    store(out_in, in_hbm.at[0])
+    store(out_in, in_hbm)
     dw_out(2)
     dw_out(1)
     for copy in started:
@@ -465,13 +476,25 @@
     assert counter[0] <= n_copies
 
 
-def write_kernel(*refs):
-    n = 4
-    copies = [pltpu.make_async_copy(refs[i], refs[n + i], refs[2 * n].at[i]) for i in range(n)]
-    for copy in copies:
-        copy.start()
-    for copy in copies:
-        copy.wait()
+def write_kernel(n, chunks, *refs):
+    sources, targets = refs[:n], refs[n : 2 * n]
+    staged = refs[2 * n : 3 * n]
+    load_sems, store_sems = refs[3 * n :]
+    steps = []
+    for a in range(n):
+        rows = staged[a].shape[0] // chunks
+        for c in range(chunks):
+            part = pl.ds(c * rows, rows)
+            i = len(steps)
+            load = pltpu.make_async_copy(sources[a].at[part], staged[a].at[part], load_sems.at[i])
+            store = pltpu.make_async_copy(staged[a].at[part], targets[a].at[part], store_sems.at[i])
+            load.start()
+            steps.append((load, store))
+    for load, store in steps:
+        load.wait()
+        store.start()
+    for _, store in steps:
+        store.wait()
 
 
 def fused_device(
@@ -538,7 +561,7 @@
         pltpu.SemaphoreType.DMA((4,)),
     ]
     grad_w = jax.ShapeDtypeStruct((feats, width), BF16)
-    shapes = (jax.ShapeDtypeStruct((1, toks, cols), BF16), grad_w, grad_w, grad_w)
+    shapes = (grad_w, grad_w, grad_w, jax.ShapeDtypeStruct((toks, cols), BF16))
     results = pl.pallas_call(
         functools.partial(fused_kernel, n_head, n_copies),
         out_shape=shapes,
@@ -561,14 +584,18 @@
         junction_counts,
         pred_grad,
     )
-    return pl.pallas_call(
-        write_kernel,
+    chunks = 4
+    out_q, out_k, out_v, out_in = pl.pallas_call(
+        functools.partial(write_kernel, 4, chunks),
         out_shape=shapes,
         in_specs=[hbm] * 4,
         out_specs=(hbm,) * 4,
-        scratch_shapes=[pltpu.SemaphoreType.DMA((4,))],
+        scratch_shapes=[pltpu.VMEM(s.shape, s.dtype) for s in shapes]
+        + [pltpu.SemaphoreType.DMA((4 * chunks,)), pltpu.SemaphoreType.DMA((4 * chunks,))],
+        compiler_params=pltpu.CompilerParams(vmem_limit_bytes=16 * 1024 * 1024),
         name="write_results",
     )(*results)
+    return out_in[None], out_q, out_k, out_v
 
 
 def on_device(

time: 175 us -> 71 us (0.41)
  Pallas kernels: 174 us -> 65.4 us
  local copies, waits for them, and re-layouts: 0 us -> 4.73 us
    pallas_call x1, Pallas kernels: 114 us -> 3.08 us  [fused_device(): pl.pallas_call(functools.partial(write_kernel, 4, chunks), out_shape=shap...]
    unnamed x0 -> x8, local copies, waits for them, and re-layouts: none -> 4.73 us
    pallas_call x1, Pallas kernels: 60.1 us -> 62.3 us  [fused_device(): pl.pallas_call(functools.partial(fused_kernel, n_head, n_copies), out_sha...]
where the time goes in v3:
time: 71 us; the launch traced here: 70.8 us
  Pallas kernels  65.4 us (92%)
  local copies, waits for them, and re-layouts  4.73 us (7%)
    pallas_call x1, Pallas kernels, fused_device(): pl.pallas_call(functools.partial(fused_kernel, n_head, n_copies), out_sha...  62.3 us
    unnamed x8, local copies, waits for them, and re-layouts  4.73 us
    pallas_call x1, Pallas kernels, fused_device(): pl.pallas_call(functools.partial(write_kernel, 4, chunks), out_shape=shap...  3.08 us

profile of v3, /device:TPU:0, one launch (start us, length us, event | category | flops | bytes accessed | tf_op | source)
XLA Modules:
  0.0 70.8 jit_solution(12540020410192156828)
XLA Ops:
  0.6 62.3 %attention_backward.1 = (bf16[384,1536]{1,0:T(8,128)(2,1)}, bf16[384,1536]{1,0:T(8,128)(2,1)}, bf16[384,1536]{1,0:T(8,128)(2,1)}, bf16[256,384]{1,0:T(8,128)(2,1)}) custom-call(bf16[1,256,1536]{2,1,0:T(8,128)(2,1)} %hid_hbm.1, bf16[1,256,384]{2,1,0:T(8,128)(2,1)} %ctx_hbm.1, bf16[384,1536]{1,0:T(8,128)(2,1)} %wq_hbm.1, bf16[384,1536]{1,0:T(8,128)(2,1)} %wk_hbm.1, ...), custom_call_target="tpu_custom_call" | custom-call | tf_op jit(solution)/shard_map/attention_backward/pallas_call | solution.py:565
  62.9 0.0 copy-start
  62.9 1.3 %copy-done = bf16[384,1536]{1,0:T(8,128)(2,1)S(1)} copy-done((bf16[384,1536]{1,0:T(8,128)(2,1)S(1)}, bf16[384,1536]{1,0:T(8,128)(2,1)}, u32[]{:S(2)}) %copy-start) | copy-done | bytes 1179672
  64.2 0.0 copy-start.1
  64.2 1.3 %copy-done.1 = bf16[384,1536]{1,0:T(8,128)(2,1)S(1)} copy-done((bf16[384,1536]{1,0:T(8,128)(2,1)S(1)}, bf16[384,1536]{1,0:T(8,128)(2,1)}, u32[]{:S(2)}) %copy-start.1) | copy-done | bytes 1179672
  65.5 0.0 copy-start.2
  65.5 1.3 %copy-done.2 = bf16[384,1536]{1,0:T(8,128)(2,1)S(1)} copy-done((bf16[384,1536]{1,0:T(8,128)(2,1)S(1)}, bf16[384,1536]{1,0:T(8,128)(2,1)}, u32[]{:S(2)}) %copy-start.2) | copy-done | bytes 1179672
  66.8 0.0 copy-start.3
  66.8 0.9 %copy-done.3 = bf16[256,384]{1,0:T(8,128)(2,1)S(1)} copy-done((bf16[256,384]{1,0:T(8,128)(2,1)S(1)}, bf16[256,384]{1,0:T(8,128)(2,1)}, u32[]{:S(2)}) %copy-start.3) | copy-done | bytes 196632
  67.7 3.1 %write_results.1 = (bf16[384,1536]{1,0:T(8,128)(2,1)}, bf16[384,1536]{1,0:T(8,128)(2,1)}, bf16[384,1536]{1,0:T(8,128)(2,1)}, bf16[256,384]{1,0:T(8,128)(2,1)}) custom-call(bf16[384,1536]{1,0:T(8,128)(2,1)S(1)} %copy-done, bf16[384,1536]{1,0:T(8,128)(2,1)S(1)} %copy-done.1, bf16[384,1536]{1,0:T(8,128)(2,1)S(1)} %copy-done.2, bf16[256,384]{1,0:T(8,128)(2,1)S(1)} %copy-done.3), custom_call_target="tpu_custom_call" | custom-call | tf_op jit(solution)/shard_map/write_results/pallas_call | solution.py:588
Async XLA Ops:
  62.9 1.3 %copy-start = (bf16[384,1536]{1,0:T(8,128)(2,1)S(1)}, bf16[384,1536]{1,0:T(8,128)(2,1)}, u32[]{:S(2)}) copy-start(bf16[384,1536]{1,0:T(8,128)(2,1)} %get-tuple-element.12.refs_0_) | copy-start | bytes 3538948
  64.2 1.3 %copy-start.1 = (bf16[384,1536]{1,0:T(8,128)(2,1)S(1)}, bf16[384,1536]{1,0:T(8,128)(2,1)}, u32[]{:S(2)}) copy-start(bf16[384,1536]{1,0:T(8,128)(2,1)} %get-tuple-element.13.refs_1_) | copy-start | bytes 3538948
  65.5 1.3 %copy-start.2 = (bf16[384,1536]{1,0:T(8,128)(2,1)S(1)}, bf16[384,1536]{1,0:T(8,128)(2,1)}, u32[]{:S(2)}) copy-start(bf16[384,1536]{1,0:T(8,128)(2,1)} %get-tuple-element.14.refs_2_) | copy-start | bytes 3538948
  66.8 0.9 %copy-start.3 = (bf16[256,384]{1,0:T(8,128)(2,1)S(1)}, bf16[256,384]{1,0:T(8,128)(2,1)}, u32[]{:S(2)}) copy-start(bf16[256,384]{1,0:T(8,128)(2,1)} %get-tuple-element.15.refs_3_) | copy-start | bytes 589828

commit v4 on v3

--- a/solution.py
+++ b/solution.py
@@ -58,6 +58,7 @@
     fbuf,
     slotbuf,
     qbuf,
+    ctx_h,
     q_t,
     ctx_t,
     sref,
@@ -176,7 +177,8 @@
     v_sib = send(vbuf.at[0], vbuf.at[1], sib)
     loads[3].wait()
     q_full = dot_nt(hid[...], wq[...])
-    qbuf[...] = q_full.astype(BF16)
+    for h in range(heads):
+        qbuf[h] = q_full[:, h * HD : (h + 1) * HD].astype(BF16)
     q_t[...] = jnp.transpose(q_full).astype(BF16)
     loads[4].wait()
     fbuf[0] = dot_nn(hid[...], wj[...]).astype(BF16)
@@ -214,15 +216,17 @@
 
     def scores(r):
         for h in range(heads):
-            sref[h, :, block_cols(r)] = dot_nt(qbuf[:, head_cols(h)], kbuf[r, :, head_cols(h)])
+            sref[h, :, block_cols(r)] = dot_nt(qbuf[h], kbuf[r, :, head_cols(h)])
 
     def dprobs(r):
         for h in range(heads):
-            dpref[h, :, block_cols(r)] = dot_nt(ctx[:, head_cols(h)], vbuf[r, :, head_cols(h)])
+            dpref[h, :, block_cols(r)] = dot_nt(ctx_h[h], vbuf[r, :, head_cols(h)])
 
     scores(0)
     loads[5].wait()
     ctx_t[...] = jnp.transpose(ctx[...].astype(F32)).astype(BF16)
+    for h in range(heads):
+        ctx_h[h] = ctx[:, head_cols(h)]
     dprobs(0)
     k_sib.wait_recv()
     scores(1)
@@ -232,18 +236,19 @@
     k_fw.wait_recv()
     scores(3)
 
-    rows_step = 32
-
-    for h in range(heads):
-
-        @pl.loop(0, toks // rows_step)
-        def _(i, h=h):
-            rows = pl.ds(pl.multiple_of(i * rows_step, rows_step), rows_step)
-            raw = sref[h, rows, :] * scale
-            e = jnp.exp(raw - jnp.max(raw, axis=-1, keepdims=True))
-            p = e / jnp.sum(e, axis=-1, keepdims=True)
-            sref[h, rows, :] = p
-            pb[h, rows, :] = p.astype(BF16)
+    rows_step = 16
+
+    @pl.loop(0, toks // rows_step)
+    def _(i):
+        rows = pl.ds(pl.multiple_of(i * rows_step, rows_step), rows_step)
+        raws = [sref[h, rows, :] * scale for h in range(heads)]
+        tops = [jnp.max(raw, axis=-1, keepdims=True) for raw in raws]
+        es = [jnp.exp(raw - top) for raw, top in zip(raws, tops)]
+        sums = [jnp.sum(e, axis=-1, keepdims=True) for e in es]
+        ps = [e * (1.0 / total) for e, total in zip(es, sums)]
+        for h in range(heads):
+            sref[h, rows, :] = ps[h]
+            pb[h, rows, :] = ps[h].astype(BF16)
 
     def kv_terms(which, left_t, right, factor):
         def one(h, r):
@@ -308,15 +313,14 @@
     v_fw.wait_recv()
     dprobs(3)
 
-    for h in range(heads):
-
-        @pl.loop(0, toks // rows_step)
-        def _(i, h=h):
-            rows = pl.ds(pl.multiple_of(i * rows_step, rows_step), rows_step)
-            p = sref[h, rows, :]
-            dp = dpref[h, rows, :]
-            delta = jnp.sum(p * dp, axis=-1, keepdims=True)
-            dsb[h, rows, :] = (p * (dp - delta)).astype(BF16)
+    @pl.loop(0, toks // rows_step)
+    def _(i):
+        rows = pl.ds(pl.multiple_of(i * rows_step, rows_step), rows_step)
+        ps = [sref[h, rows, :] for h in range(heads)]
+        dps = [dpref[h, rows, :] for h in range(heads)]
+        deltas = [jnp.sum(p * dp, axis=-1, keepdims=True) for p, dp in zip(ps, dps)]
+        for h in range(heads):
+            dsb[h, rows, :] = (ps[h] * (dps[h] - deltas[h])).astype(BF16)
 
     k_pend = kv_terms(0, q_t, dsb, scale)
 
@@ -433,25 +437,28 @@
     )
     grad_feat = grad_feat.astype(BF16)
 
+    cols = width // n_head
+
+    def owner_lanes(d):
+        owner = lax.rem(hd + d, n_head) if d > 0 else hd
+        return pl.ds(pl.multiple_of(owner * cols, 128), cols)
+
+    for d in range(n_head):
+        lanes = owner_lanes(d)
+        acc = dot_nn(grads[0], wq[:, lanes]) + dot_nn(grads[2], wv[:, lanes])
+        zown[d] = acc + dot_nt(grad_feat, wj[lanes, :])
+
     kv_final(0, 1, *k_pend)
+    z_copy = []
+    far_first = [2, 1, 3] if n_head == 4 else list(range(n_head - 1, 0, -1))
+    for d in far_first:
+        block = zown[d] + dot_nn(grads[1], wk[:, owner_lanes(d)])
+        zsend[d - 1] = block.astype(BF16)
+        z_copy.append((d, send(zsend.at[d - 1], zrecv.at[d - 1], zpeers[d - 1])))
+    dw_start(1)
     dw_final(0)
-    dw_start(1)
-
-    cols = width // n_head
-    z_copy = []
-
-    def input_block(owner):
-        lanes = pl.ds(pl.multiple_of(owner * cols, 128), cols)
-        acc = dot_nn(grads[0], wq[:, lanes]) + dot_nn(grads[1], wk[:, lanes])
-        acc = acc + dot_nn(grads[2], wv[:, lanes])
-        return acc + dot_nt(grad_feat, wj[lanes, :])
-
-    for d in range(n_head - 1, 0, -1):
-        zsend[d - 1] = input_block(lax.rem(hd + d, n_head)).astype(BF16)
-        z_copy.append((d, send(zsend.at[d - 1], zrecv.at[d - 1], zpeers[d - 1])))
-        if d == n_head - 1:
-            dw_final(2)
-    zown[...] = input_block(hd)
+    zown[0] = zown[0] + dot_nn(grads[1], wk[:, owner_lanes(0)])
+    dw_final(2)
     dw_forward(0)
     dw_final(1)
     dw_forward(2)
@@ -462,7 +469,7 @@
     dw_last(1)
     for d, copy in z_copy:
         copy.wait_recv()
-    total = zown[...]
+    total = zown[0]
     for d in range(n_head - 1):
         total = total + zrecv[d].astype(F32)
     out_in[...] = total.astype(BF16)
@@ -535,7 +542,8 @@
         pltpu.VMEM((4, toks, feats), BF16),
         pltpu.VMEM((4, toks, PJ), BF16),
         pltpu.VMEM((4, 8, n_slots), F32),
-        pltpu.VMEM((toks, feats), BF16),
+        pltpu.VMEM((heads, toks, HD), BF16),
+        pltpu.VMEM((heads, toks, HD), BF16),
         pltpu.VMEM((feats, toks), BF16),
         pltpu.VMEM((feats, toks), BF16),
         pltpu.VMEM((heads, toks, 4 * toks), F32),
@@ -554,7 +562,7 @@
         pltpu.VMEM((3, 2, feats // 8, half), BF16),
         pltpu.VMEM((n_head - 1, toks, cols), BF16),
         pltpu.VMEM((n_head - 1, toks, cols), BF16),
-        pltpu.VMEM((toks, cols), F32),
+        pltpu.VMEM((n_head, toks, cols), F32),
         pltpu.SemaphoreType.DMA((n_copies,)),
         pltpu.SemaphoreType.DMA((n_copies,)),
         pltpu.SemaphoreType.DMA((6,)),
@@ -592,7 +600,7 @@
         out_specs=(hbm,) * 4,
         scratch_shapes=[pltpu.VMEM(s.shape, s.dtype) for s in shapes]
         + [pltpu.SemaphoreType.DMA((4 * chunks,)), pltpu.SemaphoreType.DMA((4 * chunks,))],
-        compiler_params=pltpu.CompilerParams(vmem_limit_bytes=16 * 1024 * 1024),
+        compiler_params=pltpu.CompilerParams(vmem_limit_bytes=56 * 1024 * 1024),
         name="write_results",
     )(*results)
     return out_in[None], out_q, out_k, out_v

time: 71 us -> 69 us (0.972)
  local copies, waits for them, and re-layouts: 4.73 us -> 0 us
  Pallas kernels: 65.4 us -> 68 us
    unnamed x8 -> x0, local copies, waits for them, and re-layouts: 4.73 us -> none
    pallas_call x1, Pallas kernels: 62.3 us -> 64.8 us  [fused_device(): pl.pallas_call(functools.partial(fused_kernel, n_head, n_copies), out_sha...]
where the time goes in v4:
time: 69 us; the launch traced here: 68.6 us
  Pallas kernels  68 us (99%)
    pallas_call x1, Pallas kernels, fused_device(): pl.pallas_call(functools.partial(fused_kernel, n_head, n_copies), out_sha...  64.8 us
    pallas_call x1, Pallas kernels, fused_device(): pl.pallas_call(functools.partial(write_kernel, 4, chunks), out_shape=shap...  3.2 us

profile of v4, /device:TPU:0, one launch (start us, length us, event | category | flops | bytes accessed | tf_op | source)
XLA Modules:
  0.0 68.6 jit_solution(8065795597278006724)
XLA Ops:
  0.6 64.8 %attention_backward.1 = (bf16[384,1536]{1,0:T(8,128)(2,1)}, bf16[384,1536]{1,0:T(8,128)(2,1)}, bf16[384,1536]{1,0:T(8,128)(2,1)}, bf16[256,384]{1,0:T(8,128)(2,1)}) custom-call(bf16[1,256,1536]{2,1,0:T(8,128)(2,1)} %hid_hbm.1, bf16[1,256,384]{2,1,0:T(8,128)(2,1)} %ctx_hbm.1, bf16[384,1536]{1,0:T(8,128)(2,1)} %wq_hbm.1, bf16[384,1536]{1,0:T(8,128)(2,1)} %wk_hbm.1, ...), custom_call_target="tpu_custom_call" | custom-call | tf_op jit(solution)/shard_map/attention_backward/pallas_call | solution.py:573
  65.4 3.2 %write_results.1 = (bf16[384,1536]{1,0:T(8,128)(2,1)}, bf16[384,1536]{1,0:T(8,128)(2,1)}, bf16[384,1536]{1,0:T(8,128)(2,1)}, bf16[256,384]{1,0:T(8,128)(2,1)}) custom-call(bf16[384,1536]{1,0:T(8,128)(2,1)} %get-tuple-element.12.refs_0_, bf16[384,1536]{1,0:T(8,128)(2,1)} %get-tuple-element.13.refs_1_, bf16[384,1536]{1,0:T(8,128)(2,1)} %get-tuple-element.14.refs_2_, ...), custom_call_target="tpu_custom_call" | custom-call | tf_op jit(solution)/shard_map/write_results/pallas_call | solution.py:596

commit v5 on v4

--- a/solution.py
+++ b/solution.py
@@ -118,10 +118,10 @@
     for i, (src, dst) in enumerate(
         (
             (hid_hbm.at[0], hid),
+            (wj_hbm, wj),
             (wk_hbm, wk),
             (wv_hbm, wv),
             (wq_hbm, wq),
-            (wj_hbm, wj),
             (ctx_hbm.at[0], ctx),
         )
     ):
@@ -161,8 +161,12 @@
 
     loads[0].wait()
     loads[1].wait()
+    fbuf[0] = dot_nn(hid[...], wj[...]).astype(BF16)
+    loads[2].wait()
     kbuf[0] = dot_nt(hid[...], wk[...]).astype(BF16)
     pl.semaphore_wait(barrier, len(peers))
+    f_xn = send(fbuf.at[0, z_rows(0)], fbuf.at[2, z_rows(0)], xn)
+    f_sib = send(fbuf.at[0], fbuf.at[1], sib)
     k_xn = send(kbuf.at[0], kbuf.at[2], xn)
     k_sib = send(kbuf.at[0], kbuf.at[1], sib)
     hid_yn = []
@@ -171,20 +175,6 @@
         hid_yn.append(
             send(hidbuf.at[z_rows(0), lanes], hidbuf.at[z_rows(2 * toks), lanes], yn)
         )
-    loads[2].wait()
-    vbuf[0] = dot_nt(hid[...], wv[...]).astype(BF16)
-    v_xn = send(vbuf.at[0], vbuf.at[2], xn)
-    v_sib = send(vbuf.at[0], vbuf.at[1], sib)
-    loads[3].wait()
-    q_full = dot_nt(hid[...], wq[...])
-    for h in range(heads):
-        qbuf[h] = q_full[:, h * HD : (h + 1) * HD].astype(BF16)
-    q_t[...] = jnp.transpose(q_full).astype(BF16)
-    loads[4].wait()
-    fbuf[0] = dot_nn(hid[...], wj[...]).astype(BF16)
-    f_xn = send(fbuf.at[0, z_rows(0)], fbuf.at[2, z_rows(0)], xn)
-    f_sib = send(fbuf.at[0], fbuf.at[1], sib)
-
     n_acc, slot_dev = donor.shape[2], donor.shape[3]
     n_slots = slotbuf.shape[2]
     acc_iota = lax.broadcasted_iota(jnp.int32, (n_acc, slot_dev), 0)
@@ -206,6 +196,15 @@
         slotbuf[0, i : i + 1, :] = jnp.sum(spread, axis=0, keepdims=True)
     t_xn = send(slotbuf.at[0], slotbuf.at[2], xn)
     t_sib = send(slotbuf.at[0], slotbuf.at[1], sib)
+    loads[3].wait()
+    vbuf[0] = dot_nt(hid[...], wv[...]).astype(BF16)
+    v_xn = send(vbuf.at[0], vbuf.at[2], xn)
+    v_sib = send(vbuf.at[0], vbuf.at[1], sib)
+    loads[4].wait()
+    q_full = dot_nt(hid[...], wq[...])
+    for h in range(heads):
+        qbuf[h] = q_full[:, h * HD : (h + 1) * HD].astype(BF16)
+    q_t[...] = jnp.transpose(q_full).astype(BF16)
     hid_sib = send(hidbuf.at[0:toks], hidbuf.at[toks : 2 * toks], sib)
 
     def head_cols(h):
@@ -222,192 +221,26 @@
         for h in range(heads):
             dpref[h, :, block_cols(r)] = dot_nt(ctx_h[h], vbuf[r, :, head_cols(h)])
 
+    def pass_on(arrived, ref):
+        arrived.wait_recv()
+        return send(ref, ref, zpair)
+
+    def hid_lanes(p):
+        return slice(p * half, (p + 1) * half)
+
+    f_z = pass_on(f_xn, fbuf.at[2, z_rows(0)])
+    t_xn.wait_recv()
+    t_fw = send(slotbuf.at[2], slotbuf.at[3], sib)
     scores(0)
     loads[5].wait()
     ctx_t[...] = jnp.transpose(ctx[...].astype(F32)).astype(BF16)
     for h in range(heads):
         ctx_h[h] = ctx[:, head_cols(h)]
     dprobs(0)
+    f_z.wait_recv()
+    f_fw = send(fbuf.at[2], fbuf.at[3], sib)
     k_sib.wait_recv()
     scores(1)
-    k_xn.wait_recv()
-    k_fw = send(kbuf.at[2], kbuf.at[3], sib)
-    scores(2)
-    k_fw.wait_recv()
-    scores(3)
-
-    rows_step = 16
-
-    @pl.loop(0, toks // rows_step)
-    def _(i):
-        rows = pl.ds(pl.multiple_of(i * rows_step, rows_step), rows_step)
-        raws = [sref[h, rows, :] * scale for h in range(heads)]
-        tops = [jnp.max(raw, axis=-1, keepdims=True) for raw in raws]
-        es = [jnp.exp(raw - top) for raw, top in zip(raws, tops)]
-        sums = [jnp.sum(e, axis=-1, keepdims=True) for e in es]
-        ps = [e * (1.0 / total) for e, total in zip(es, sums)]
-        for h in range(heads):
-            sref[h, rows, :] = ps[h]
-            pb[h, rows, :] = ps[h].astype(BF16)
-
-    def kv_terms(which, left_t, right, factor):
-        def one(h, r):
-            part = dot_nn(left_t[head_cols(h), :], right[h, :, block_cols(r)])
-            return part * factor if factor != 1.0 else part
-
-        for h in range(heads):
-            term[which, 0, head_cols(h), :] = one(h, 3).astype(BF16)
-        a = send(term.at[which, 0], from_sib.at[which, 0], sib)
-        for h in range(heads):
-            term[which, 1, head_cols(h), :] = one(h, 1).astype(BF16)
-        b = send(term.at[which, 1], from_sib.at[which, 1], sib)
-        for h in range(heads):
-            own_term[which, head_cols(h), :] = one(h, 2)
-        a.wait_recv()
-        pair_sum[which] = (own_term[which] + from_sib[which, 0].astype(F32)).astype(BF16)
-        c = send(pair_sum.at[which], from_xn.at[which], xn)
-        for h in range(heads):
-            own_term[which, head_cols(h), :] = one(h, 0)
-        return b, c
-
-    def g_rows(y, c):
-        return pl.ds(pl.multiple_of(y * row_y + c * row_c, 16), row_c)
-
-    g_copy = [None] * 3
-
-    def exchange(slot):
-        gcat[slot, :, 0:toks] = grads_t[slot, g_rows(iv, core), :]
-        copies = []
-        for b, dev, y, c in ((2, yn, 1 - iv, core), (3, ysib, 1 - iv, 1 - core), (1, sib, iv, 1 - core)):
-            copies.append(
-                send(grads_t.at[slot, g_rows(y, c)], gcat.at[slot, :, block_cols(b)], dev)
-            )
-        g_copy[slot] = copies
-
-    def kv_final(which, slot, b, c):
-        b.wait_recv()
-        c.wait_recv()
-        total = own_term[which] + from_sib[which, 1].astype(F32) + from_xn[which].astype(F32)
-        grads_t[slot] = total.astype(BF16)
-        exchange(slot)
-        grads[slot] = jnp.transpose(total).astype(BF16)
-
-    def pass_on(arrived, ref):
-        arrived.wait_recv()
-        return send(ref, ref, zpair)
-
-    def hid_lanes(p):
-        return slice(p * half, (p + 1) * half)
-
-    hid_z = [pass_on(hid_yn[0], hidbuf.at[z_rows(2 * toks), hid_lanes(0)])]
-    v_pend = kv_terms(1, ctx_t, pb, 1.0)
-    v_sib.wait_recv()
-    dprobs(1)
-    v_xn.wait_recv()
-    v_fw = send(vbuf.at[2], vbuf.at[3], sib)
-    hid_z.append(pass_on(hid_yn[1], hidbuf.at[z_rows(2 * toks), hid_lanes(1)]))
-    f_z = pass_on(f_xn, fbuf.at[2, z_rows(0)])
-    t_xn.wait_recv()
-    t_fw = send(slotbuf.at[2], slotbuf.at[3], sib)
-    dprobs(2)
-    v_fw.wait_recv()
-    dprobs(3)
-
-    @pl.loop(0, toks // rows_step)
-    def _(i):
-        rows = pl.ds(pl.multiple_of(i * rows_step, rows_step), rows_step)
-        ps = [sref[h, rows, :] for h in range(heads)]
-        dps = [dpref[h, rows, :] for h in range(heads)]
-        deltas = [jnp.sum(p * dp, axis=-1, keepdims=True) for p, dp in zip(ps, dps)]
-        for h in range(heads):
-            dsb[h, rows, :] = (ps[h] * (dps[h] - deltas[h])).astype(BF16)
-
-    k_pend = kv_terms(0, q_t, dsb, scale)
-
-    q_parts = []
-    for h in range(heads):
-        acc = dot_nn(dsb[h, :, block_cols(0)], kbuf[0, :, head_cols(h)])
-        for r in range(1, 4):
-            acc = acc + dot_nn(dsb[h, :, block_cols(r)], kbuf[r, :, head_cols(h)])
-        q_parts.append(acc * scale)
-    q_grad = jnp.concatenate(q_parts, axis=-1)
-    grads_t[0] = jnp.transpose(q_grad).astype(BF16)
-    exchange(0)
-    grads[0] = q_grad.astype(BF16)
-
-    f_z.wait_recv()
-    f_fw = send(fbuf.at[2], fbuf.at[3], sib)
-    hid_fw = []
-    for p in range(2):
-        lanes = hid_lanes(p)
-        hid_z[p].wait_recv()
-        hid_fw.append(
-            send(hidbuf.at[2 * toks : 3 * toks, lanes], hidbuf.at[3 * toks : 4 * toks, lanes], sib)
-        )
-
-    outs = (out_q, out_k, out_v)
-    outs_hbm = (q_hbm, k_hbm, v_hbm)
-    rs_copy = {}
-    piece_copy = {}
-    fwd_copy = {}
-    sib_copy = {0: [], 1: [], 2: []}
-
-    def x_rows(x):
-        return pl.ds(pl.multiple_of(x * row_x, 16), row_x)
-
-    def piece(w, p, y, x):
-        start = pl.multiple_of(y * row_y + core * row_c + x * row_x, 16)
-        return outs[w].at[pl.ds(start, row_x), slice(p * half, (p + 1) * half)]
-
-    def to_sib(w, ref):
-        sib_copy[w].append(send(ref, ref, sib))
-
-    def dw_start(w):
-        for copy in g_copy[w]:
-            copy.wait_recv()
-        for p in range(2):
-            dwp[w, p] = dot_nn(gcat[w], hidbuf[:, p * half : (p + 1) * half]).astype(BF16)
-            rs_copy[w, p] = send(dwp.at[w, p, x_rows(1 - xi)], rsum.at[w, p], xn)
-
-    def dw_final(w):
-        for p in range(2):
-            rs_copy[w, p].wait_recv()
-            done = dwp[w, p, x_rows(xi), :].astype(F32) + rsum[w, p].astype(F32)
-            ref = piece(w, p, iv, xi)
-            ref[...] = done.astype(BF16)
-            cx = send(ref, ref, xn)
-            cy = send(ref, ref, yn)
-            piece_copy[w, p] = (cx, cy)
-            to_sib(w, ref)
-
-    def dw_forward(w):
-        for p in range(2):
-            cx = piece_copy[w, p][0]
-            cx_ref = piece(w, p, iv, 1 - xi)
-            cx.wait_recv()
-            fwd_copy[w, p] = send(cx_ref, cx_ref, yn)
-            to_sib(w, cx_ref)
-        for p in range(2):
-            piece_copy[w, p][1].wait_recv()
-            to_sib(w, piece(w, p, 1 - iv, xi))
-
-    def dw_last(w):
-        for p in range(2):
-            fwd_copy[w, p].wait_recv()
-            to_sib(w, piece(w, p, 1 - iv, 1 - xi))
-
-    def dw_out(w):
-        for copy in sib_copy[w]:
-            copy.wait_recv()
-        store(outs[w], outs_hbm[w])
-
-    kv_final(1, 2, *v_pend)
-    hid_sib.wait_recv()
-    hid_fw[0].wait_recv()
-    hid_fw[1].wait_recv()
-    dw_start(0)
-    dw_start(2)
-
     f_sib.wait_recv()
     t_sib.wait_recv()
     f_fw.wait_recv()
@@ -437,39 +270,213 @@
     )
     grad_feat = grad_feat.astype(BF16)
 
+    k_xn.wait_recv()
+    k_fw = send(kbuf.at[2], kbuf.at[3], sib)
+    scores(2)
+    k_fw.wait_recv()
+    scores(3)
+
+    rows_step = 16
+
+    @pl.loop(0, toks // rows_step)
+    def _(i):
+        rows = pl.ds(pl.multiple_of(i * rows_step, rows_step), rows_step)
+        raws = [sref[h, rows, :] * scale for h in range(heads)]
+        tops = [jnp.max(raw, axis=-1, keepdims=True) for raw in raws]
+        es = [jnp.exp(raw - top) for raw, top in zip(raws, tops)]
+        sums = [jnp.sum(e, axis=-1, keepdims=True) for e in es]
+        ps = [e * (1.0 / total) for e, total in zip(es, sums)]
+        for h in range(heads):
+            sref[h, rows, :] = ps[h]
+            pb[h, rows, :] = ps[h].astype(BF16)
+
+    def kv_terms(which, left_t, right, factor):
+        def one(h, r):
+            part = dot_nn(left_t[head_cols(h), :], right[h, :, block_cols(r)])
+            return part * factor if factor != 1.0 else part
+
+        for h in range(heads):
+            term[which, 0, head_cols(h), :] = one(h, 3).astype(BF16)
+        a = send(term.at[which, 0], from_sib.at[which, 0], sib)
+        for h in range(heads):
+            term[which, 1, head_cols(h), :] = one(h, 1).astype(BF16)
+        b = send(term.at[which, 1], from_sib.at[which, 1], sib)
+        for h in range(heads):
+            own_term[which, head_cols(h), :] = one(h, 2)
+        a.wait_recv()
+        pair_sum[which] = (own_term[which] + from_sib[which, 0].astype(F32)).astype(BF16)
+        c = send(pair_sum.at[which], from_xn.at[which], xn)
+        for h in range(heads):
+            own_term[which, head_cols(h), :] = one(h, 0)
+        return b, c
+
+    def g_rows(y, c):
+        return pl.ds(pl.multiple_of(y * row_y + c * row_c, 16), row_c)
+
+    g_copy = [None] * 3
+
+    def exchange(slot):
+        gcat[slot, :, 0:toks] = grads_t[slot, g_rows(iv, core), :]
+        copies = []
+        for b, dev, y, c in ((2, yn, 1 - iv, core), (3, ysib, 1 - iv, 1 - core), (1, sib, iv, 1 - core)):
+            copies.append(
+                send(grads_t.at[slot, g_rows(y, c)], gcat.at[slot, :, block_cols(b)], dev)
+            )
+        g_copy[slot] = copies
+
+    def kv_final(which, slot, b, c):
+        b.wait_recv()
+        c.wait_recv()
+        total = own_term[which] + from_sib[which, 1].astype(F32) + from_xn[which].astype(F32)
+        grads_t[slot] = total.astype(BF16)
+        exchange(slot)
+
+    hid_z = [pass_on(hid_yn[0], hidbuf.at[z_rows(2 * toks), hid_lanes(0)])]
+    v_pend = kv_terms(1, ctx_t, pb, 1.0)
+    v_sib.wait_recv()
+    dprobs(1)
+    v_xn.wait_recv()
+    v_fw = send(vbuf.at[2], vbuf.at[3], sib)
+    hid_z.append(pass_on(hid_yn[1], hidbuf.at[z_rows(2 * toks), hid_lanes(1)]))
+    dprobs(2)
+    v_fw.wait_recv()
+    dprobs(3)
+
+    @pl.loop(0, toks // rows_step)
+    def _(i):
+        rows = pl.ds(pl.multiple_of(i * rows_step, rows_step), rows_step)
+        ps = [sref[h, rows, :] for h in range(heads)]
+        dps = [dpref[h, rows, :] for h in range(heads)]
+        deltas = [jnp.sum(p * dp, axis=-1, keepdims=True) for p, dp in zip(ps, dps)]
+        for h in range(heads):
+            dsb[h, rows, :] = (ps[h] * (dps[h] - deltas[h])).astype(BF16)
+
+    k_pend = kv_terms(0, q_t, dsb, scale)
+
+    q_parts = []
+    for h in range(heads):
+        acc = dot_nn(dsb[h, :, block_cols(0)], kbuf[0, :, head_cols(h)])
+        for r in range(1, 4):
+            acc = acc + dot_nn(dsb[h, :, block_cols(r)], kbuf[r, :, head_cols(h)])
+        q_parts.append(acc * scale)
+    q_grad = jnp.concatenate(q_parts, axis=-1)
+    grads_t[0] = jnp.transpose(q_grad).astype(BF16)
+    exchange(0)
+    grads[0] = q_grad.astype(BF16)
+
+    hid_fw = []
+    for p in range(2):
+        lanes = hid_lanes(p)
+        hid_z[p].wait_recv()
+        hid_fw.append(
+            send(hidbuf.at[2 * toks : 3 * toks, lanes], hidbuf.at[3 * toks : 4 * toks, lanes], sib)
+        )
+
+    outs = (out_q, out_k, out_v)
+    outs_hbm = (q_hbm, k_hbm, v_hbm)
+    rs_copy = {}
+    piece_copy = {}
+    fwd_copy = {}
+    sib_copy = {0: [], 1: [], 2: []}
+
+    def x_rows(x):
+        return pl.ds(pl.multiple_of(x * row_x, 16), row_x)
+
+    def piece(w, p, y, x):
+        start = pl.multiple_of(y * row_y + core * row_c + x * row_x, 16)
+        return outs[w].at[pl.ds(start, row_x), slice(p * half, (p + 1) * half)]
+
+    def to_sib(w, ref):
+        sib_copy[w].append(send(ref, ref, sib))
+
+    def dw_start(w):
+        for copy in g_copy[w]:
+            copy.wait_recv()
+        for p in range(2):
+            dwp[w, p] = dot_nn(gcat[w], hidbuf[:, p * half : (p + 1) * half]).astype(BF16)
+            rs_copy[w, p] = send(dwp.at[w, p, x_rows(1 - xi)], rsum.at[w, p], xn)
+
+    def dw_final(w):
+        for p in range(2):
+            rs_copy[w, p].wait_recv()
+            done = dwp[w, p, x_rows(xi), :].astype(F32) + rsum[w, p].astype(F32)
+            ref = piece(w, p, iv, xi)
+            ref[...] = done.astype(BF16)
+            cx = send(ref, ref, xn)
+            cy = send(ref, ref, yn)
+            piece_copy[w, p] = (cx, cy)
+            to_sib(w, ref)
+
+    def dw_forward(w):
+        for p in range(2):
+            cx, cy = piece_copy[w, p]
+            cx_ref = piece(w, p, iv, 1 - xi)
+            cy_ref = piece(w, p, 1 - iv, xi)
+            first, ref, dev = ((cx, cx_ref, yn), (cy, cy_ref, xn))[p]
+            first.wait_recv()
+            fwd_copy[w, p] = send(ref, ref, dev)
+            to_sib(w, ref)
+        for p in range(2):
+            cx, cy = piece_copy[w, p]
+            if p == 0:
+                cy.wait_recv()
+                to_sib(w, piece(w, p, 1 - iv, xi))
+            else:
+                cx.wait_recv()
+                to_sib(w, piece(w, p, iv, 1 - xi))
+
+    def dw_last(w):
+        for p in range(2):
+            fwd_copy[w, p].wait_recv()
+            to_sib(w, piece(w, p, 1 - iv, 1 - xi))
+
+    def dw_out(w):
+        for copy in sib_copy[w]:
+            copy.wait_recv()
+        store(outs[w], outs_hbm[w])
+
+    kv_final(1, 2, *v_pend)
+    hid_sib.wait_recv()
+    hid_fw[0].wait_recv()
+    hid_fw[1].wait_recv()
+    dw_start(0)
+    kv_final(0, 1, *k_pend)
+    dw_start(2)
+    dw_final(0)
+    dw_start(1)
+    for slot in (1, 2):
+        grads[slot] = jnp.transpose(grads_t[slot].astype(F32)).astype(BF16)
+    dw_final(2)
+
     cols = width // n_head
-
-    def owner_lanes(d):
+    z_copy = []
+
+    def input_block(d):
         owner = lax.rem(hd + d, n_head) if d > 0 else hd
-        return pl.ds(pl.multiple_of(owner * cols, 128), cols)
-
-    for d in range(n_head):
-        lanes = owner_lanes(d)
-        acc = dot_nn(grads[0], wq[:, lanes]) + dot_nn(grads[2], wv[:, lanes])
-        zown[d] = acc + dot_nt(grad_feat, wj[lanes, :])
-
-    kv_final(0, 1, *k_pend)
-    z_copy = []
-    far_first = [2, 1, 3] if n_head == 4 else list(range(n_head - 1, 0, -1))
-    for d in far_first:
-        block = zown[d] + dot_nn(grads[1], wk[:, owner_lanes(d)])
-        zsend[d - 1] = block.astype(BF16)
+        lanes = pl.ds(pl.multiple_of(owner * cols, 128), cols)
+        acc = dot_nn(grads[0], wq[:, lanes]) + dot_nn(grads[1], wk[:, lanes])
+        acc = acc + dot_nn(grads[2], wv[:, lanes])
+        return acc + dot_nt(grad_feat, wj[lanes, :])
+
+    def input_send(d):
+        zsend[d - 1] = input_block(d).astype(BF16)
         z_copy.append((d, send(zsend.at[d - 1], zrecv.at[d - 1], zpeers[d - 1])))
-    dw_start(1)
-    dw_final(0)
-    zown[0] = zown[0] + dot_nn(grads[1], wk[:, owner_lanes(0)])
-    dw_final(2)
+
+    input_send(2)
+    dw_final(1)
+    input_send(1)
     dw_forward(0)
-    dw_final(1)
+    input_send(3)
     dw_forward(2)
+    zown[...] = input_block(0)
+    dw_forward(1)
     dw_last(0)
-    dw_forward(1)
     dw_last(2)
     dw_out(0)
     dw_last(1)
     for d, copy in z_copy:
         copy.wait_recv()
-    total = zown[0]
+    total = zown[...]
     for d in range(n_head - 1):
         total = total + zrecv[d].astype(F32)
     out_in[...] = total.astype(BF16)
@@ -562,7 +569,7 @@
         pltpu.VMEM((3, 2, feats // 8, half), BF16),
         pltpu.VMEM((n_head - 1, toks, cols), BF16),
         pltpu.VMEM((n_head - 1, toks, cols), BF16),
-        pltpu.VMEM((n_head, toks, cols), F32),
+        pltpu.VMEM((toks, cols), F32),
         pltpu.SemaphoreType.DMA((n_copies,)),
         pltpu.SemaphoreType.DMA((n_copies,)),
         pltpu.SemaphoreType.DMA((6,)),

time: 69 us -> 67.9 us (0.984)
  Pallas kernels: 68 us -> 67.1 us
    pallas_call x1, Pallas kernels: 64.8 us -> 63.9 us  [fused_device(): pl.pallas_call(functools.partial(fused_kernel, n_head, n_copies), out_sha...]
where the time goes in v5:
time: 67.9 us; the launch traced here: 67.7 us
  Pallas kernels  67.1 us (99%)
    pallas_call x1, Pallas kernels, fused_device(): pl.pallas_call(functools.partial(fused_kernel, n_head, n_copies), out_sha...  63.9 us
    pallas_call x1, Pallas kernels, fused_device(): pl.pallas_call(functools.partial(write_kernel, 4, chunks), out_shape=shap...  3.2 us

profile of v5, /device:TPU:0, one launch (start us, length us, event | category | flops | bytes accessed | tf_op | source)
XLA Modules:
  0.0 67.7 jit_solution(904266328791235676)
XLA Ops:
  0.6 63.9 %attention_backward.1 = (bf16[384,1536]{1,0:T(8,128)(2,1)}, bf16[384,1536]{1,0:T(8,128)(2,1)}, bf16[384,1536]{1,0:T(8,128)(2,1)}, bf16[256,384]{1,0:T(8,128)(2,1)}) custom-call(bf16[1,256,1536]{2,1,0:T(8,128)(2,1)} %hid_hbm.1, bf16[1,256,384]{2,1,0:T(8,128)(2,1)} %ctx_hbm.1, bf16[384,1536]{1,0:T(8,128)(2,1)} %wq_hbm.1, bf16[384,1536]{1,0:T(8,128)(2,1)} %wk_hbm.1, ...), custom_call_target="tpu_custom_call" | custom-call | tf_op jit(solution)/shard_map/attention_backward/pallas_call | solution.py:580
  64.5 3.2 %write_results.1 = (bf16[384,1536]{1,0:T(8,128)(2,1)}, bf16[384,1536]{1,0:T(8,128)(2,1)}, bf16[384,1536]{1,0:T(8,128)(2,1)}, bf16[256,384]{1,0:T(8,128)(2,1)}) custom-call(bf16[384,1536]{1,0:T(8,128)(2,1)} %get-tuple-element.12.refs_0_, bf16[384,1536]{1,0:T(8,128)(2,1)} %get-tuple-element.13.refs_1_, bf16[384,1536]{1,0:T(8,128)(2,1)} %get-tuple-element.14.refs_2_, ...), custom_call_target="tpu_custom_call" | custom-call | tf_op jit(solution)/shard_map/write_results/pallas_call | solution.py:603

commit v6 on v5

--- a/solution.py
+++ b/solution.py
@@ -39,20 +39,16 @@
     accept,
     counts,
     pred,
-    q_hbm,
-    k_hbm,
-    v_hbm,
-    in_hbm,
+    out_q,
+    out_k,
+    out_v,
+    out_in,
     hidbuf,
     ctx,
     wq,
     wk,
     wv,
     wj,
-    out_in,
-    out_q,
-    out_k,
-    out_v,
     kbuf,
     vbuf,
     fbuf,
@@ -81,7 +77,6 @@
     send_sems,
     recv_sems,
     load_sems,
-    store_sems,
 ):
     toks = ctx.shape[0]
     width = hidbuf.shape[1]
@@ -146,13 +141,6 @@
         copy.start()
         started.append(copy)
         return copy
-
-    stores = []
-
-    def store(src, dst):
-        copy = pltpu.make_async_copy(src, dst, store_sems.at[len(stores)])
-        copy.start()
-        stores.append(copy)
 
     barrier = pltpu.get_barrier_semaphore()
     peers = [sib, xn, yn, ysib] + zpeers
@@ -205,7 +193,6 @@
     for h in range(heads):
         qbuf[h] = q_full[:, h * HD : (h + 1) * HD].astype(BF16)
     q_t[...] = jnp.transpose(q_full).astype(BF16)
-    hid_sib = send(hidbuf.at[0:toks], hidbuf.at[toks : 2 * toks], sib)
 
     def head_cols(h):
         return slice(h * HD, (h + 1) * HD)
@@ -303,12 +290,17 @@
         b = send(term.at[which, 1], from_sib.at[which, 1], sib)
         for h in range(heads):
             own_term[which, head_cols(h), :] = one(h, 2)
+        return a, b
+
+    def kv_cross(which, a):
         a.wait_recv()
         pair_sum[which] = (own_term[which] + from_sib[which, 0].astype(F32)).astype(BF16)
-        c = send(pair_sum.at[which], from_xn.at[which], xn)
+        return send(pair_sum.at[which], from_xn.at[which], xn)
+
+    def kv_own(which, left_t, right, factor):
         for h in range(heads):
-            own_term[which, head_cols(h), :] = one(h, 0)
-        return b, c
+            part = dot_nn(left_t[head_cols(h), :], right[h, :, block_cols(0)])
+            own_term[which, head_cols(h), :] = part * factor if factor != 1.0 else part
 
     def g_rows(y, c):
         return pl.ds(pl.multiple_of(y * row_y + c * row_c, 16), row_c)
@@ -332,11 +324,13 @@
         exchange(slot)
 
     hid_z = [pass_on(hid_yn[0], hidbuf.at[z_rows(2 * toks), hid_lanes(0)])]
-    v_pend = kv_terms(1, ctx_t, pb, 1.0)
+    v_a, v_b = kv_terms(1, ctx_t, pb, 1.0)
     v_sib.wait_recv()
     dprobs(1)
+    v_c = kv_cross(1, v_a)
     v_xn.wait_recv()
     v_fw = send(vbuf.at[2], vbuf.at[3], sib)
+    hid_sib = send(hidbuf.at[0:toks], hidbuf.at[toks : 2 * toks], sib)
     hid_z.append(pass_on(hid_yn[1], hidbuf.at[z_rows(2 * toks), hid_lanes(1)]))
     dprobs(2)
     v_fw.wait_recv()
@@ -351,7 +345,7 @@
         for h in range(heads):
             dsb[h, rows, :] = (ps[h] * (dps[h] - deltas[h])).astype(BF16)
 
-    k_pend = kv_terms(0, q_t, dsb, scale)
+    k_a, k_b = kv_terms(0, q_t, dsb, scale)
 
     q_parts = []
     for h in range(heads):
@@ -359,6 +353,7 @@
         for r in range(1, 4):
             acc = acc + dot_nn(dsb[h, :, block_cols(r)], kbuf[r, :, head_cols(h)])
         q_parts.append(acc * scale)
+    k_c = kv_cross(0, k_a)
     q_grad = jnp.concatenate(q_parts, axis=-1)
     grads_t[0] = jnp.transpose(q_grad).astype(BF16)
     exchange(0)
@@ -373,7 +368,6 @@
         )
 
     outs = (out_q, out_k, out_v)
-    outs_hbm = (q_hbm, k_hbm, v_hbm)
     rs_copy = {}
     piece_copy = {}
     fwd_copy = {}
@@ -433,14 +427,15 @@
     def dw_out(w):
         for copy in sib_copy[w]:
             copy.wait_recv()
-        store(outs[w], outs_hbm[w])
-
-    kv_final(1, 2, *v_pend)
+
+    kv_own(1, ctx_t, pb, 1.0)
+    kv_final(1, 2, v_b, v_c)
+    kv_own(0, q_t, dsb, scale)
     hid_sib.wait_recv()
     hid_fw[0].wait_recv()
     hid_fw[1].wait_recv()
     dw_start(0)
-    kv_final(0, 1, *k_pend)
+    kv_final(0, 1, k_b, k_c)
     dw_start(2)
     dw_final(0)
     dw_start(1)
@@ -480,35 +475,20 @@
     for d in range(n_head - 1):
         total = total + zrecv[d].astype(F32)
     out_in[...] = total.astype(BF16)
-    store(out_in, in_hbm)
     dw_out(2)
     dw_out(1)
     for copy in started:
         copy.wait_send()
-    for copy in stores:
+    assert counter[0] <= n_copies
+
+
+def write_kernel(n, *refs):
+    sems = refs[2 * n]
+    copies = [pltpu.make_async_copy(refs[i], refs[n + i], sems.at[i]) for i in range(n)]
+    for copy in copies:
+        copy.start()
+    for copy in copies:
         copy.wait()
-    assert counter[0] <= n_copies
-
-
-def write_kernel(n, chunks, *refs):
-    sources, targets = refs[:n], refs[n : 2 * n]
-    staged = refs[2 * n : 3 * n]
-    load_sems, store_sems = refs[3 * n :]
-    steps = []
-    for a in range(n):
-        rows = staged[a].shape[0] // chunks
-        for c in range(chunks):
-            part = pl.ds(c * rows, rows)
-            i = len(steps)
-            load = pltpu.make_async_copy(sources[a].at[part], staged[a].at[part], load_sems.at[i])
-            store = pltpu.make_async_copy(staged[a].at[part], targets[a].at[part], store_sems.at[i])
-            load.start()
-            steps.append((load, store))
-    for load, store in steps:
-        load.wait()
-        store.start()
-    for _, store in steps:
-        store.wait()
 
 
 def fused_device(
@@ -541,10 +521,6 @@
         pltpu.VMEM((feats, width), BF16),
         pltpu.VMEM((feats, width), BF16),
         pltpu.VMEM((width, PJ), BF16),
-        pltpu.VMEM((toks, cols), BF16),
-        pltpu.VMEM((feats, width), BF16),
-        pltpu.VMEM((feats, width), BF16),
-        pltpu.VMEM((feats, width), BF16),
         pltpu.VMEM((4, toks, feats), BF16),
         pltpu.VMEM((4, toks, feats), BF16),
         pltpu.VMEM((4, toks, PJ), BF16),
@@ -573,18 +549,17 @@
         pltpu.SemaphoreType.DMA((n_copies,)),
         pltpu.SemaphoreType.DMA((n_copies,)),
         pltpu.SemaphoreType.DMA((6,)),
-        pltpu.SemaphoreType.DMA((4,)),
     ]
     grad_w = jax.ShapeDtypeStruct((feats, width), BF16)
     shapes = (grad_w, grad_w, grad_w, jax.ShapeDtypeStruct((toks, cols), BF16))
     results = pl.pallas_call(
         functools.partial(fused_kernel, n_head, n_copies),
-        out_shape=shapes,
+        out_shape=tuple(pltpu.VMEM(s.shape, s.dtype) for s in shapes),
         in_specs=[hbm] * 6 + [vmem] * 4,
-        out_specs=(hbm,) * 4,
+        out_specs=(vmem,) * 4,
         scratch_shapes=scratch,
         compiler_params=pltpu.CompilerParams(
-            collective_id=0, has_side_effects=True, vmem_limit_bytes=56 * 1024 * 1024
+            collective_id=0, has_side_effects=True, vmem_limit_bytes=59 * 1024 * 1024
         ),
         name="attention_backward",
     )(
@@ -599,15 +574,13 @@
         junction_counts,
         pred_grad,
     )
-    chunks = 4
     out_q, out_k, out_v, out_in = pl.pallas_call(
-        functools.partial(write_kernel, 4, chunks),
+        functools.partial(write_kernel, 4),
         out_shape=shapes,
-        in_specs=[hbm] * 4,
+        in_specs=[vmem] * 4,
         out_specs=(hbm,) * 4,
-        scratch_shapes=[pltpu.VMEM(s.shape, s.dtype) for s in shapes]
-        + [pltpu.SemaphoreType.DMA((4 * chunks,)), pltpu.SemaphoreType.DMA((4 * chunks,))],
-        compiler_params=pltpu.CompilerParams(vmem_limit_bytes=56 * 1024 * 1024),
+        scratch_shapes=[pltpu.SemaphoreType.DMA((4,))],
+        compiler_params=pltpu.CompilerParams(vmem_limit_bytes=16 * 1024 * 1024),
         name="write_results",
     )(*results)
     return out_in[None], out_q, out_k, out_v

time: 67.9 us -> 64.9 us (0.956)
  Pallas kernels: 67.1 us -> 64.1 us
    pallas_call x1, Pallas kernels: 63.9 us -> 62.2 us  [fused_device(): pl.pallas_call(functools.partial(fused_kernel, n_head, n_copies), out_sha...]
    pallas_call x1, Pallas kernels: 3.2 us -> 1.88 us  [fused_device(): pl.pallas_call(functools.partial(write_kernel, 4), out_shape=shapes, in_s...]
where the time goes in v6:
time: 64.9 us; the launch traced here: 64.7 us
  Pallas kernels  64.1 us (99%)
    pallas_call x1, Pallas kernels, fused_device(): pl.pallas_call(functools.partial(fused_kernel, n_head, n_copies), out_sha...  62.2 us
    pallas_call x1, Pallas kernels, fused_device(): pl.pallas_call(functools.partial(write_kernel, 4), out_shape=shapes, in_s...  1.88 us

profile of v6, /device:TPU:0, one launch (start us, length us, event | category | flops | bytes accessed | tf_op | source)
XLA Modules:
  0.0 64.7 jit_solution(14230445536247871323)
XLA Ops:
  0.6 62.2 %attention_backward.1 = (bf16[384,1536]{1,0:T(8,128)(2,1)S(1)}, bf16[384,1536]{1,0:T(8,128)(2,1)S(1)}, bf16[384,1536]{1,0:T(8,128)(2,1)S(1)}, bf16[256,384]{1,0:T(8,128)(2,1)S(1)}) custom-call(bf16[1,256,1536]{2,1,0:T(8,128)(2,1)} %hid_hbm.1, bf16[1,256,384]{2,1,0:T(8,128)(2,1)} %ctx_hbm.1, bf16[384,1536]{1,0:T(8,128)(2,1)} %wq_hbm.1, ...), custom_call_target="tpu_custom_call" | custom-call | tf_op jit(solution)/shard_map/attention_backward/pallas_call | solution.py:555
  62.9 1.9 %write_results.1 = (bf16[384,1536]{1,0:T(8,128)(2,1)}, bf16[384,1536]{1,0:T(8,128)(2,1)}, bf16[384,1536]{1,0:T(8,128)(2,1)}, bf16[256,384]{1,0:T(8,128)(2,1)}) custom-call(bf16[384,1536]{1,0:T(8,128)(2,1)S(1)} %get-tuple-element.12.refs_0_, bf16[384,1536]{1,0:T(8,128)(2,1)S(1)} %get-tuple-element.13.refs_1_, ...), custom_call_target="tpu_custom_call" | custom-call | tf_op jit(solution)/shard_map/write_results/pallas_call | solution.py:577

commit v7 on v6

--- a/solution.py
+++ b/solution.py
@@ -458,14 +458,14 @@
         z_copy.append((d, send(zsend.at[d - 1], zrecv.at[d - 1], zpeers[d - 1])))
 
     input_send(2)
+    dw_forward(0)
     dw_final(1)
     input_send(1)
-    dw_forward(0)
+    dw_forward(2)
     input_send(3)
-    dw_forward(2)
+    dw_last(0)
+    dw_forward(1)
     zown[...] = input_block(0)
-    dw_forward(1)
-    dw_last(0)
     dw_last(2)
     dw_out(0)
     dw_last(1)

time: 64.9 us -> 64.9 us (level)
  no operation moved by 1% of the time
where the time goes in v7:
time: 64.9 us; the launch traced here: 64.7 us
  Pallas kernels  64.1 us (99%)
    pallas_call x1, Pallas kernels, fused_device(): pl.pallas_call(functools.partial(fused_kernel, n_head, n_copies), out_sha...  62.2 us
    pallas_call x1, Pallas kernels, fused_device(): pl.pallas_call(functools.partial(write_kernel, 4), out_shape=shapes, in_s...  1.88 us

profile of v7, /device:TPU:0, one launch (start us, length us, event | category | flops | bytes accessed | tf_op | source)
XLA Modules:
  0.0 64.7 jit_solution(4293240944604370898)
XLA Ops:
  0.6 62.2 %attention_backward.1 = (bf16[384,1536]{1,0:T(8,128)(2,1)S(1)}, bf16[384,1536]{1,0:T(8,128)(2,1)S(1)}, bf16[384,1536]{1,0:T(8,128)(2,1)S(1)}, bf16[256,384]{1,0:T(8,128)(2,1)S(1)}) custom-call(bf16[1,256,1536]{2,1,0:T(8,128)(2,1)} %hid_hbm.1, bf16[1,256,384]{2,1,0:T(8,128)(2,1)} %ctx_hbm.1, bf16[384,1536]{1,0:T(8,128)(2,1)} %wq_hbm.1, ...), custom_call_target="tpu_custom_call" | custom-call | tf_op jit(solution)/shard_map/attention_backward/pallas_call | solution.py:555
  62.9 1.9 %write_results.1 = (bf16[384,1536]{1,0:T(8,128)(2,1)}, bf16[384,1536]{1,0:T(8,128)(2,1)}, bf16[384,1536]{1,0:T(8,128)(2,1)}, bf16[256,384]{1,0:T(8,128)(2,1)}) custom-call(bf16[384,1536]{1,0:T(8,128)(2,1)S(1)} %get-tuple-element.12.refs_0_, bf16[384,1536]{1,0:T(8,128)(2,1)S(1)} %get-tuple-element.13.refs_1_, ...), custom_call_target="tpu_custom_call" | custom-call | tf_op jit(solution)/shard_map/write_results/pallas_call | solution.py:577
